TPU v7x, 32 devices: a whole 2x2x4 slice. The times are simulated.
32 devices in a mesh: depth: 4 (over y, x), track: 8 (over z, core).
Axes of the slice: x: 2, y: 2, z: 4, core: 2. Of those that a mesh axis runs over, the one named last changes fastest.
Arguments:
- slowness_cells: float32 [128, 16384], P('depth'), may hold values from 0.5 to 2
- cell_of_group: int32 [128], P('track'), may hold values from 0 to 16383
- taper: float32 [256, 9], replicated, may hold values from 0 to 0.25
- secant: float32 [256], replicated, may hold values from 1 to 3
- primary: bfloat16 [128, 4096, 256], P('depth', 'track'), may hold values from -0.3984375 to 0.3984375
- quadrature: bfloat16 [128, 4096, 256], P('depth', 'track'), may hold values from -0.3984375 to 0.3984375
- observed: float32 [128, 4096], P('depth', 'track'), may hold values from -6 to 6
Outputs:
- focused: float32 [128, 4096], P('depth', 'track')
- gradient: float32 [128, 16384], P('depth')
All inputs are finite; a program needn't handle non-finite values.
Results may differ from a plain program's by a relative error of at most 0.0003.
Values sent between devices are 32-bit elements; how exact they have to be, the bound alone decides.
No kernel may reach another device: no remote copies, remote signals or barrier semaphores. Data moves between devices by JAX's collectives and lax.ppermute only.
A program may use at most 128 MiB of HBM per device.

v0:
```python
import jax
import jax.numpy as jnp
from jax import lax
from jax.sharding import PartitionSpec as P

OMEGA = 0.25


def with_halo(block, sides, width):
    for axis, dim in sides:
        count = lax.axis_size(axis)
        forward = [(i, i + 1) for i in range(count - 1)]
        backward = [(target, source) for source, target in forward]
        low = lax.ppermute(
            lax.slice_in_dim(block, block.shape[dim] - width, None, axis=dim), axis, forward
        )
        high = lax.ppermute(lax.slice_in_dim(block, 0, width, axis=dim), axis, backward)
        block = jnp.concatenate([low, block, high], axis=dim)
    return block


def entering(value, axis, join, neutral, backward):
    count, mine = (lax.axis_size(axis), lax.axis_index(axis))
    pieces = lax.all_gather(value, axis)
    if backward:
        pieces = pieces[::-1]
        mine = count - 1 - mine
    running = jnp.full_like(value, 0) + jnp.asarray(neutral, value.dtype)

    def hop(position, running):
        longer = join(running, pieces[position])
        return jnp.where(position < mine, longer, running)

    return lax.fori_loop(0, count - 1, hop, running)


def adding(earlier, later):
    return earlier + later


def on_device(slowness_cells, cell_of_group, taper, secant, primary, quadrature, observed):
    taps = taper.shape[1]
    reach = (taps - 1) // 2
    traces = primary.shape[1]
    nlocal = cell_of_group.shape[0]
    group = traces // nlocal
    high = lax.Precision.HIGHEST
    cells = jnp.repeat(cell_of_group, group)
    slow = jnp.take(slowness_cells, cells, axis=1)
    rimmed = with_halo(slow, (("track", 1),), reach)
    window = jnp.stack([rimmed[:, k : k + traces] for k in range(taps)], 0)
    increment = jnp.einsum("kzx,ak->zxa", window, taper, precision=high) * secant
    local = jnp.cumsum(increment, axis=0)
    zeros = jnp.zeros(local.shape[1:], jnp.float32)
    above = entering(local[-1], "depth", adding, zeros, False)
    travel = local + above
    cosine = jnp.cos(OMEGA * travel)
    sine = jnp.sin(OMEGA * travel)
    prim = primary.astype(jnp.float32)
    quad = quadrature.astype(jnp.float32)
    focused = jnp.sum(prim * cosine + quad * sine, axis=2)
    resid = focused - observed
    time_grad = OMEGA * resid[:, :, None] * (quad * cosine - prim * sine)
    deeper = jnp.flip(jnp.cumsum(jnp.flip(time_grad, 0), axis=0), 0)
    below = entering(deeper[0], "depth", adding, zeros, True)
    step_grad = deeper + below
    spread = jnp.einsum("zxa,ak->kzx", step_grad * secant, taper, precision=high)
    spread = with_halo(spread, (("track", 2),), reach)
    slow_grad = jnp.zeros(slow.shape, jnp.float32)
    for k in range(taps):
        slow_grad = slow_grad + spread[k, :, 2 * reach - k : 2 * reach - k + traces]
    group_sums = jnp.sum(slow_grad.reshape(slow_grad.shape[0], nlocal, group), axis=2)
    ncells = slowness_cells.shape[1]
    all_sums, all_cells = (
        lax.all_gather(group_sums, "track", axis=1, tiled=True),
        lax.all_gather(cell_of_group, "track", axis=0, tiled=True),
    )
    gradient = jax.ops.segment_sum(all_sums.T, all_cells.astype(jnp.int32), num_segments=ncells).T
    return (focused, gradient)


def solution(mesh):
    in_specs = (
        P("depth", None),
        P("track"),
        P(),
        P(),
        P("depth", "track", None),
        P("depth", "track", None),
        P("depth", "track"),
    )
    out_specs = (P("depth", "track"), P("depth", None))
    return jax.shard_map(
        on_device, mesh=mesh, in_specs=in_specs, out_specs=out_specs, check_vma=False
    )
```

profile of v0, /device:TPU:0, one launch (start us, length us, event | category | flops | bytes accessed | tf_op | source)
XLA Modules:
  0.0 362.6 jit_solution(5015419848236085226)
XLA Ops:
  8.1 6.3 %copy.32 = f32[32,16384]{0,1:T(8,128)} copy(f32[32,16384]{1,0:T(8,128)} %param.11) | data formatting | bytes 4194304 | tf_op args[0]
  14.4 4.4 %gather_fusion = f32[512,32]{1,0:T(8,128)S(1)} fusion(f32[32,16384]{0,1:T(8,128)} %copy.32, s32[1024]{0:T(1024)S(1)} %pad_clamp_fusion), kind=kCustom, calls=%fused_computation | custom fusion | bytes 133120 | tf_op jit(solution)/shard_map/jit(_take)/gather | solution.py:49
  19.0 2.3 collective-permute-start
  21.4 1.3 collective-permute-start.1
  22.8 3.9 %collective-permute-done.1 = f32[32,4]{1,0:T(8,128)S(1)} collective-permute-done((f32[32,4]{1,0:T(8,128)S(1)}, f32[32,4]{1,0:T(8,128)S(1)}, u32[]{:S(2)}, u32[]{:S(2)}) %collective-permute-start.1) | collective-permute-done | bytes 544 | tf_op jit(solution)/shard_map/ppermute | solution.py:17
  27.5 1.0 stack.36
  28.5 15.9 %fusion.37 = f32[32,512,256]{2,1,0:T(8,128)} fusion(f32[9,32,512]{2,0,1:T(8,128)S(1)} %stack.36, f32[256,9]{0,1:T(8,128)S(1)} %copy-done), kind=kOutput, calls=%fused_computation.69 | convolution fusion | flops 452984832 | bytes 17376256 | tf_op jit(solution)/shard_map/kzx,ak->zxa/dot_general | solution.py:52
  44.4 6.7 %fusion.7 = f32[32,512,256]{2,1,0:T(8,128)S(1)} fusion(f32[32,512,256]{2,1,0:T(8,128)} %fusion.37, f32[256]{0:T(256)S(1)} %copy-done.5), kind=kOutput, calls=%fused_computation.16 | output fusion | flops 134217728 | bytes 33555456 | tf_op jit(solution)/shard_map/jit(cumsum)/reduce_window_sum | solution.py:53
  51.1 5.7 %copy-done.1 = f32[32,512,256]{2,1,0:T(8,128)} copy-done((f32[32,512,256]{2,1,0:T(8,128)}, f32[32,512,256]{2,1,0:T(8,128)S(1)}, u32[]{:S(2)}) %copy-start.1) | copy-done | bytes 16777240
  56.8 0.8 slice.125
  57.9 37.6 %all-gather.3.cloned.1.call-done = f32[4,512,256]{2,1,0:T(8,128)} async-done(((f32[1,512,256]{2,1,0:T(8,128)}), f32[4,512,256]{2,1,0:T(8,128)}) %all-gather.3.cloned.1.call-update) | async-done | bytes 2097168 | tf_op jit(solution)/shard_map/all_gather | solution.py:24
  95.5 3.7 %while.28 = (s32[]{:T(128)}, f32[512,256]{1,0:T(8,128)S(1)}, s32[]{:T(128)}, f32[4,512,256]{2,1,0:T(8,128)}, s32[]{:T(128)}, /*index=5*/s32[]{:T(128)}) while((s32[]{:T(128)}, f32[512,256]{1,0:T(8,128)S(1)}, s32[]{:T(128)}, f32[4,512,256]{2,1,0:T(8,128)}, s32[]{:T(128)}, /*index=5*/s32[]{:T(128)}) %tuple.78), condition=%wide.region_2.3_spmd.clone, body=%wide.region_1.2_spmd.clone.sunk | while | flops 393220 | bytes 1572957 | solution.py:34
  95.5 1.2 add_select_fusion.4
  96.7 1.2 add_select_fusion.4
  98.0 1.2 add_select_fusion.4
  99.2 66.9 %fusion.1 = f32[32,512]{1,0:T(8,128)S(1)} fusion(bf16[32,512,256]{2,1,0:T(8,128)(2,1)} %param.15, bf16[32,512,256]{2,1,0:T(8,128)(2,1)} %param.16, f32[32,512,256]{2,1,0:T(8,128)} %copy-done.1, f32[512,256]{1,0:T(8,128)S(1)} %get-tuple-element.160), kind=kLoop, calls=%fused_computation.9 | loop fusion | flops 33538048 | bytes 34144256 | tf_op jit(solution)/shard_map/reduce_sum | solution.py:61
  166.1 66.8 %fusion.3 = f32[32,512,256]{2,1,0:T(8,128)} fusion(bf16[32,512,256]{2,1,0:T(8,128)(2,1)} %param.15, bf16[32,512,256]{2,1,0:T(8,128)(2,1)} %param.16, f32[32,512,256]{2,1,0:T(8,128)} %copy-done.1, f32[32,512]{1,0:T(8,128)S(1)} %subtract_multiply_fusion, f32[512,256]{1,0:T(8,128)S(1)} %get-tuple-element.160), kind=kLoop, calls=%fused_computation.11 | loop fusion | flops 33554432 | bytes 50921472 | tf_op jit(solution)/shard_map/mul | solution.py:63
  232.9 11.3 %rev.10 = f32[32,512,256]{2,1,0:T(8,128)} reverse(f32[32,512,256]{2,1,0:T(8,128)} %fusion.3), dimensions={0} | reverse | bytes 33554432 | tf_op jit(solution)/shard_map/jit(_flip)/rev | solution.py:64
  244.2 6.7 %fusion.41 = f32[32,512,256]{2,1,0:T(8,128)S(1)} fusion(f32[32,512,256]{2,1,0:T(8,128)} %rev.10), kind=kOutput, calls=%fused_computation.77 | output fusion | flops 130023424 | bytes 33554432 | tf_op jit(solution)/shard_map/jit(cumsum)/reduce_window_sum | solution.py:64
  251.0 5.7 %copy-done.2 = f32[32,512,256]{2,1,0:T(8,128)} copy-done((f32[32,512,256]{2,1,0:T(8,128)}, f32[32,512,256]{2,1,0:T(8,128)S(1)}, u32[]{:S(2)}) %copy-start.2) | copy-done | bytes 16777240
  256.7 0.8 slice.126
  257.5 11.3 %rev.11 = f32[32,512,256]{2,1,0:T(8,128)} reverse(f32[32,512,256]{2,1,0:T(8,128)} %copy-done.2), dimensions={0} | reverse | bytes 33554432 | tf_op jit(solution)/shard_map/jit(_flip)/rev | solution.py:64
  268.9 24.1 %all-gather.5.cloned.1.call-done = f32[4,512,256]{2,1,0:T(8,128)} async-done(((f32[1,512,256]{2,1,0:T(8,128)}), f32[4,512,256]{2,1,0:T(8,128)}) %all-gather.5.cloned.1.call-update) | async-done | bytes 2097168 | tf_op jit(solution)/shard_map/all_gather | solution.py:24
  293.0 1.7 rev.12
  295.3 18.5 %fusion.16 = f32[9,32,512]{2,0,1:T(8,128)S(1)} fusion(f32[32,512,256]{2,1,0:T(8,128)} %rev.11, f32[512,256]{1,0:T(8,128)S(1)} %get-tuple-element.161, f32[256]{0:T(256)S(1)} %copy-done.5, f32[256,9]{0,1:T(8,128)S(1)} %copy-done), kind=kOutput, calls=%fused_computation.25 | convolution fusion | flops 461373440 | bytes 17901568 | tf_op jit(solution)/shard_map/zxa,ak->kzx/dot_general | solution.py:67
  313.9 1.5 collective-permute-start.2
  315.5 3.0 collective-permute-start.3
  320.0 8.9 %all-reduce = s32[128]{0:T(128)S(1)} all-reduce(s32[128]{0:T(128)S(1)} %dynamic-update-slice), channel_id=1, replica_groups=mesh['depth'=4,'track'=8] {'track'}, use_global_device_ids=true, to_apply=%add | all-reduce | flops 128 | bytes 1024
  328.9 1.5 fusion.35
  330.8 14.0 %all_gather.15 = f32[32,128]{0,1:T(8,128)S(1)} all-gather(f32[32,16]{0,1:T(8,128)S(1)} %copy.42), channel_id=1, replica_groups=mesh['depth'=4,'track'=8] {'track'}, dimensions={1}, use_global_device_ids=true | all-gather | bytes 18432 | tf_op jit(solution)/shard_map/all_gather | solution.py:75
  344.7 4.7 %scatter_custom_fusion = f32[16384,32]{1,0:T(8,128)} fusion(s32[128]{0:T(128)S(1)} %all-reduce, f32[]{:T(128)} %constant.75.clone.1, f32[32,128]{0,1:T(8,128)S(1)} %all_gather.15), kind=kCustom, calls=%fused_computation.23 | custom fusion | flops 4096 | bytes 2162692 | tf_op jit(solution)/shard_map/scatter-add | solution.py:78
  349.5 6.2 %copy.43 = f32[32,16384]{1,0:T(8,128)} copy(f32[32,16384]{0,1:T(8,128)} %bitcast.42) | data formatting | bytes 4194304
  (55 shorter events, 4.6 us)
Async XLA Ops:
  7.2 21.3 %copy-start = (f32[256,9]{0,1:T(8,128)S(1)}, f32[256,9]{0,1:T(8,128)}, u32[]{:S(2)}) copy-start(f32[256,9]{0,1:T(8,128)} %param.13) | copy-start | bytes 27652
  7.2 88.3 %all-gather.3.cloned.1.call-start = ((), (), s32[]{:S(2)}) async-start(), calls=%async_computation | async-start | bytes 2621440 | tf_op jit(solution)/shard_map/all_gather | solution.py:24
  14.4 30.0 %copy-start.5 = (f32[256]{0:T(256)S(1)}, f32[256]{0:T(256)}, u32[]{:S(2)}) copy-start(f32[256]{0:T(256)} %param.14) | copy-start | bytes 3076
  19.0 3.8 %collective-permute-start = (f32[32,4]{1,0:T(8,128)S(1)}, f32[32,4]{1,0:T(8,128)S(1)}, u32[]{:S(2)}, u32[]{:S(2)}) collective-permute-start(f32[32,4]{1,0:T(8,128)S(1)} %get-tuple-element.229), channel_id=1, source_target_pairs={{0,1},{1,2},{2,3},{3,4},{4,5},{5,6},{6,7},{8,9},{9,10},{10,11},{11... | collective-permute-start | bytes 1544 | tf_op jit(solution)/shard_map/ppermute | solution.py:14
  21.4 5.3 %collective-permute-start.1 = (f32[32,4]{1,0:T(8,128)S(1)}, f32[32,4]{1,0:T(8,128)S(1)}, u32[]{:S(2)}, u32[]{:S(2)}) collective-permute-start(f32[32,4]{1,0:T(8,128)S(1)} %get-tuple-element.228), channel_id=1, source_target_pairs={{1,0},{2,1},{3,2},{4,3},{5,4},{6,5},{7,6},{9,8},{10,9},{11,10},{12... | collective-permute-start | bytes 1544 | tf_op jit(solution)/shard_map/ppermute | solution.py:17
  51.1 5.7 %copy-start.1 = (f32[32,512,256]{2,1,0:T(8,128)}, f32[32,512,256]{2,1,0:T(8,128)S(1)}, u32[]{:S(2)}) copy-start(f32[32,512,256]{2,1,0:T(8,128)S(1)} %fusion.7) | copy-start | bytes 50331652
  57.7 235.3 %all-gather.5.cloned.1.call-start = ((), (), s32[]{:S(2)}) async-start(), calls=%async_computation.1 | async-start | bytes 2621440 | tf_op jit(solution)/shard_map/all_gather | solution.py:24
  99.2 66.9 %copy-start.4 = (f32[32,512]{1,0:T(8,128)S(1)}, f32[32,512]{1,0:T(8,128)}, u32[]{:S(2)}) copy-start(f32[32,512]{1,0:T(8,128)} %param.17) | copy-start | bytes 196612
  166.1 66.8 %copy-start.3 = (f32[32,512]{1,0:T(8,128)}, f32[32,512]{1,0:T(8,128)S(1)}, u32[]{:S(2)}) copy-start(f32[32,512]{1,0:T(8,128)S(1)} %fusion.1) | copy-start | bytes 196612
  251.0 5.7 %copy-start.2 = (f32[32,512,256]{2,1,0:T(8,128)}, f32[32,512,256]{2,1,0:T(8,128)S(1)}, u32[]{:S(2)}) copy-start(f32[32,512,256]{2,1,0:T(8,128)S(1)} %fusion.41) | copy-start | bytes 50331652
  268.9 49.6 %copy-start.7 = (u32[32]{0:T(128)S(1)}, u32[32]{0:T(128)}, u32[]{:S(2)}) copy-start(u32[32]{0:T(128)} %constant.81) | copy-start | bytes 388
  268.9 50.9 %copy-start.6 = (s32[16]{0:T(128)S(1)}, s32[16]{0:T(128)}, u32[]{:S(2)}) copy-start(s32[16]{0:T(128)} %param.12) | copy-start | bytes 196
  313.9 15.0 %collective-permute-start.2 = (f32[9,32,4]{2,0,1:T(8,128)S(1)}, f32[9,32,4]{2,0,1:T(8,128)S(1)}, u32[]{:S(2)}, u32[]{:S(2)}) collective-permute-start(f32[9,32,4]{2,0,1:T(8,128)S(1)} %get-tuple-element.214), channel_id=1, source_target_pairs={{1,0},{2,1},{3,2},{4,3},{5,4},{6,5},{7,6},{9,8},{10,9},{11,10},{12... | collective-permute-start | bytes 13832 | tf_op jit(solution)/shard_map/ppermute | solution.py:17
  315.5 13.5 %collective-permute-start.3 = (f32[9,32,4]{2,0,1:T(8,128)S(1)}, f32[9,32,4]{2,0,1:T(8,128)S(1)}, u32[]{:S(2)}, u32[]{:S(2)}) collective-permute-start(f32[9,32,4]{2,0,1:T(8,128)S(1)} %get-tuple-element.215), channel_id=1, source_target_pairs={{0,1},{1,2},{2,3},{3,4},{4,5},{5,6},{6,7},{8,9},{9,10},{10,11},{11... | collective-permute-start | bytes 13832 | tf_op jit(solution)/shard_map/ppermute | solution.py:14
Sparse Core Ops, SparseCore 0:
  57.8 37.6 all-gather.2
  257.6 35.2 all-gather.4
where the time goes:
time: 363 us
  other arithmetic  158 us (44%)
  waiting for transfers between devices  65.6 us (18%)
  local copies, waits for them, and re-layouts  58.2 us (16%)
  matrix products  34.4 us (9%)
  blocking collectives  22.9 us (6%)
  between operations  15.1 us (4%)
  starting transfers between devices  8.46 us (2%)
    reduce_sum x1, other arithmetic, on_device(): focused = jnp.sum(prim * cosine + quad * sine, axis=2)  66.9 us
    mul x2, other arithmetic, on_device(): time_grad = OMEGA * resid[:, :, None] * (quad * cosine - prim * sine)  66.8 us
    all_gather x2, waiting for transfers between devices, entering(): pieces = lax.all_gather(value, axis)  61.7 us
    unnamed x21, local copies, waits for them, and re-layouts  24.8 us
    rev x2, local copies, waits for them, and re-layouts, on_device(): deeper = jnp.flip(jnp.cumsum(jnp.flip(time_grad, 0), axis=0), 0)  22.7 us
    dot_general x1, matrix products, on_device(): jnp.einsum('zxa,ak->kzx', step_grad * secant, taper, precision=high)  18.5 us
    dot_general x1, matrix products, on_device(): jnp.einsum('kzx,ak->zxa', window, taper, precision=high) * secant  15.9 us
    all_gather x1, blocking collectives, on_device(): lax.all_gather(group_sums, 'track', axis=1, tiled=True)  14 us
  transfers between devices with their start and end apart: 6, of which 3 were waited for; matrix products, arithmetic and copies ran while one was open for 3% of the time, Pallas kernels for 0%

commit v1 on v0

v1 whole, which is shorter than its diff:
```python
import functools
import math

import jax
import jax.numpy as jnp
from jax import lax
from jax.experimental import pallas as pl
from jax.experimental.pallas import tpu as pltpu
from jax.sharding import PartitionSpec as P

OMEGA = 0.25
LANES = 128
SUBLANES = 8
MIB = 1024 * 1024
SINE = (4.442867755889893, -7.307443141937256, 3.594787359237671, -0.7843723297119141)
COSINE = (1.4142041206359863, -6.977642059326172, 5.71523904800415, -1.728348731994629)
HIGH = lax.Precision.HIGHEST
NT = (((1,), (1,)), ((), ()))
TN = (((0,), (0,)), ((), ()))
NN = (((1,), (0,)), ((), ()))


def dot32(a, b, dims):
    return lax.dot_general(a, b, dims, precision=HIGH, preferred_element_type=jnp.float32)


def dot16(a, b, dims):
    return lax.dot_general(a, b, dims, preferred_element_type=jnp.float32)


def iota(shape, dim):
    return lax.broadcasted_iota(jnp.int32, shape, dim)


def cos_sin_turns(t):
    r = t - jnp.round(t)
    z = r * r
    s = r * (SINE[0] + z * (SINE[1] + z * (SINE[2] + z * SINE[3])))
    c = COSINE[0] + z * (COSINE[1] + z * (COSINE[2] + z * COSINE[3]))
    return 1.0 - s * s, s * c


def split(x):
    hi = x.astype(jnp.bfloat16)
    return hi, (x - hi.astype(jnp.float32)).astype(jnp.bfloat16)


def gather_kernel(nloc, cells_ref, slow_ref, cum_ref, msg_ref, buf, sems):
    depth = slow_ref.shape[0]

    def copy(g):
        start = pl.multiple_of((cells_ref[g] // LANES) * LANES, LANES)
        return pltpu.make_async_copy(slow_ref.at[:, pl.ds(start, LANES)], buf.at[g], sems.at[g])

    for g in range(nloc):
        copy(g).start()
    lane = iota((depth, LANES), 1)
    lane1 = iota((1, LANES), 1)
    slow = jnp.zeros((depth, LANES), jnp.float32)
    ids = jnp.zeros((1, LANES), jnp.int32)
    for g in range(nloc):
        copy(g).wait()
        shift = lax.rem(g + LANES - lax.rem(cells_ref[g], LANES), LANES)
        slow = jnp.where(lane == g, pltpu.roll(buf[g], shift, 1), slow)
        ids = jnp.where(lane1 == g, cells_ref[g], ids)
    lower = (iota((depth, depth), 0) >= iota((depth, depth), 1)).astype(jnp.float32)
    cum = dot32(lower, slow, NN)
    cum_ref[...] = cum
    row = iota((SUBLANES, LANES), 0)
    col = iota((SUBLANES, LANES), 1)
    pick = jnp.where(((row == 2) & (col == 0)) | ((row == 3) & (col == nloc - 1)), 1.0, 0.0)
    ends = dot32(pick, cum, NT)
    ends = jnp.concatenate([ends, jnp.zeros((SUBLANES, LANES - depth), jnp.float32)], axis=1)
    total = jnp.broadcast_to(cum[depth - 1 : depth, :], (SUBLANES, LANES))
    idrow = jnp.broadcast_to(ids.astype(jnp.float32), (SUBLANES, LANES))
    msg_ref[...] = jnp.where(row == 0, total, jnp.where(row == 1, idrow, ends))


def main_kernel(
    nloc, group, reach, ndepth, ntrack, zb,
    m_ref, cum_ref, taper_ref, sec_ref, obs_ref, p_ref, q_ref,
    foc_ref, msg_ref, ids_ref,
    c_vmem, c_smem, ct, tab, cent_f, cent_e, edge_f, edge_o, edge_n, sem,
):
    depth, traces = obs_ref.shape
    taps = taper_ref.shape[1]
    angles = taper_ref.shape[0]
    step = pl.program_id(0)
    d, t = lax.axis_index("depth"), lax.axis_index("track")
    half = reach
    slots = 2 * reach

    @pl.when(step == 0)
    def _():
        slot = iota((2 * slots, taps), 0)
        k = iota((2 * slots, taps), 1)
        i = lax.rem(slot, slots)
        near = ((i < half) & (k < reach - i)) | ((i >= half) & (k >= 2 * reach - (i - half)))
        near = near.astype(jnp.float32)
        mask = jnp.where(slot < slots, 1.0 - near, near)
        weights = dot32(mask, taper_ref[...], NT) * sec_ref[...]
        tab[0 : 2 * slots, :] = weights
        tab[2 * slots : 4 * slots, :] = weights * (OMEGA / (2 * math.pi))
        tl, tr = jnp.maximum(t - 1, 0), jnp.minimum(t + 1, ntrack - 1)
        has_l = (t > 0).astype(jnp.float32)
        has_r = (t < ntrack - 1).astype(jnp.float32)
        above = jnp.zeros((1, LANES), jnp.float32)
        left = m_ref[d * ntrack + tl, 3:4, :]
        right = m_ref[d * ntrack + tr, 2:3, :]
        lane1 = iota((1, LANES), 1)
        for e in range(ndepth - 1):
            on = (e < d).astype(jnp.float32)
            above += on * m_ref[e * ntrack + t, 0:1, :]
            l_row = m_ref[e * ntrack + tl, 0:1, :]
            r_row = m_ref[e * ntrack + tr, 0:1, :]
            left += on * jnp.sum(jnp.where(lane1 == nloc - 1, l_row, 0.0), axis=1, keepdims=True)
            right += on * jnp.sum(jnp.where(lane1 == 0, r_row, 0.0), axis=1, keepdims=True)
        row = iota((SUBLANES, LANES), 0)
        col = iota((SUBLANES, LANES), 1)
        halo = jnp.where(row == 0, left * has_l, jnp.where(row == 1, right * has_r, 0.0))
        place = ((row == 0) & (col == 0)) | ((row == 1) & (col == nloc + 1))
        halo = dot32(halo, place.astype(jnp.float32), TN)[:depth]
        own = pltpu.roll(cum_ref[...] + above, 1, 1)
        lane = iota((depth, LANES), 1)
        c_ext = jnp.where((lane >= 1) & (lane <= nloc), own, halo)
        c_vmem[...] = c_ext
        copy = pltpu.make_async_copy(c_vmem, c_smem, sem)
        copy.start()
        pick = (iota((nloc, LANES), 1) == iota((nloc, LANES), 0) + 1).astype(jnp.float32)
        ct[:, 0:depth] = dot32(pick, c_ext, NT)
        ids = [m_ref[d * ntrack + s, 1:2, :] for s in range(ntrack)]
        ids_ref[...] = jnp.concatenate(ids, axis=0).astype(jnp.int32)
        copy.wait()

    own_w, near_w = tab[0:slots, :], tab[slots : 2 * slots, :]
    own_t, near_t = tab[2 * slots : 3 * slots, :], tab[3 * slots : 4 * slots, :]
    all_w = (own_w + near_w)[0:1, :]
    all_t = (own_t + near_t)[0:1, :]
    upper = iota((slots, 1), 0) < half
    lane = iota((slots, LANES), 1)
    mine = iota((nloc, traces), 0) == iota((nloc, traces), 1) // group

    def one(zi, carry):
        z = step * zb + zi
        column = jnp.where(iota((nloc, depth), 1) == z, ct[:, 0:depth], 0.0)
        c, s = cos_sin_turns(jnp.sum(column, axis=1, keepdims=True) * all_t)
        c_hi, c_lo = split(c)
        s_hi, s_lo = split(s)
        wc_hi, wc_lo = split(all_w * c)
        ws_hi, ws_lo = split(-all_w * s)
        rows_p = jnp.concatenate([c_hi, c_lo, ws_hi, ws_lo], axis=0)
        rows_q = jnp.concatenate([s_hi, s_lo, wc_hi, wc_lo], axis=0)
        both = dot16(rows_p, p_ref[zi], NT) + dot16(rows_q, q_ref[zi], NT)
        f = jnp.where(mine, both[0:nloc] + both[nloc : 2 * nloc], 0.0)
        e = jnp.where(mine, both[2 * nloc : 3 * nloc] + both[3 * nloc :], 0.0)
        cent_f[pl.ds(z, 1), :] = jnp.sum(f, axis=0, keepdims=True)
        cent_e[pl.ds(z, 1), :] = jnp.sum(e, axis=0, keepdims=True)
        here = lane == z
        for g in range(nloc):
            near = jnp.where(upper, c_smem[z, g], c_smem[z, g + 2])
            c, s = cos_sin_turns(own_t * c_smem[z, g + 1] + near_t * near)

            def edges(ref):
                first = ref[zi, g * group : g * group + 2 * SUBLANES, :].astype(jnp.float32)
                last = ref[zi, (g + 1) * group - 2 * SUBLANES : (g + 1) * group, :].astype(jnp.float32)
                return jnp.where(upper, first[:slots], last[2 * SUBLANES - slots :])

            p, q = edges(p_ref), edges(q_ref)
            f = p * c + q * s
            dd = q * c - p * s
            at = pl.ds(g * slots, slots)
            for ref, value in ((edge_f, f), (edge_o, dd * own_w), (edge_n, dd * near_w)):
                ref[at, :] = jnp.where(here, jnp.sum(value, axis=1, keepdims=True), ref[at, :])
        return carry

    @pl.when(step == 0)
    def _():
        for ref in (edge_f, edge_o, edge_n):
            ref[...] = jnp.zeros(ref.shape, jnp.float32)

    lax.fori_loop(0, zb, one, 0)

    @pl.when(step == pl.num_programs(0) - 1)
    def _():
        count = nloc * slots
        e, x = iota((count, traces), 0), iota((count, traces), 1)
        i = lax.rem(e, slots)
        spread = x == (e // slots) * group + jnp.where(i < half, i, group - slots + i)
        spread = spread.astype(jnp.float32)
        r = lax.rem(iota((depth, traces), 1), group)
        is_edge = (r < half) | (r >= group - half)
        f_x = dot32(edge_f[...], spread, TN)[:depth]
        o_x = dot32(edge_o[...], spread, TN)[:depth]
        n_x = dot32(edge_n[...], spread, TN)[:depth]
        focused = jnp.where(is_edge, f_x, cent_f[...])
        foc_ref[...] = focused
        resid = OMEGA * (focused - obs_ref[...])
        a = resid * jnp.where(is_edge, o_x, cent_e[...])
        b = resid * n_x
        x, lane_g = iota((traces, LANES), 0), iota((traces, LANES), 1)
        r, g = lax.rem(x, group), x // group
        to_own = (lane_g == g + 1).astype(jnp.float32)
        to_near = ((r < half) & (lane_g == g)) | ((r >= group - half) & (lane_g == g + 2))
        sums = dot32(a, to_own, NN) + dot32(b, to_near.astype(jnp.float32), NN)
        later = (iota((depth, depth), 1) >= iota((depth, depth), 0)).astype(jnp.float32)
        sums = dot32(later, sums, NN)
        parts = depth // SUBLANES
        width = LANES // parts
        lane8 = iota((SUBLANES, LANES), 1)
        packed = jnp.zeros((SUBLANES, LANES), jnp.float32)
        for part in range(parts):
            piece = sums[part * SUBLANES : (part + 1) * SUBLANES]
            piece = piece if part == 0 else pltpu.roll(piece, part * width, 1)
            packed = jnp.where(lane8 // width == part, piece, packed)
        msg_ref[...] = packed


def scatter_kernel(nloc, ndepth, ntrack, m_ref, ids_ref, out_ref):
    depth = out_ref.shape[0]
    d = lax.axis_index("depth")
    parts = depth // SUBLANES
    width = LANES // parts
    lane = iota((depth, LANES), 1)
    out_ref[...] = jnp.zeros(out_ref.shape, jnp.float32)

    def segment(s, carry):
        packed = m_ref[d * ntrack + s]
        pieces = [packed] + [pltpu.roll(packed, LANES - k * width, 1) for k in range(1, parts)]
        below = jnp.zeros((1, LANES), jnp.float32)
        for e in range(1, ndepth):
            below += (e > d).astype(jnp.float32) * m_ref[e * ntrack + s, 0:1, :]
        sums = jnp.concatenate(pieces, axis=0) + below
        for j in range(nloc + 2):
            if j == 0:
                cell, on = ids_ref[jnp.maximum(s - 1, 0), nloc - 1], s > 0
            elif j == nloc + 1:
                cell, on = ids_ref[jnp.minimum(s + 1, ntrack - 1), 0], s < ntrack - 1
            else:
                cell, on = ids_ref[s, j - 1], True
            at = lax.rem(cell, LANES)
            start = pl.multiple_of((cell // LANES) * LANES, LANES)
            moved = pltpu.roll(sums, lax.rem(at + LANES - j, LANES), 1)
            hit = lane == jnp.where(on, at, -1)
            out_ref[:, pl.ds(start, LANES)] += jnp.where(hit, moved, 0.0)
        return carry

    lax.fori_loop(0, ntrack, segment, 0)


def whole(shape):
    return pl.BlockSpec(shape, lambda *_: (0,) * len(shape))


def on_device(slowness_cells, cell_of_group, taper, secant, primary, quadrature, observed):
    ndepth, ntrack = lax.axis_size("depth"), lax.axis_size("track")
    ndev = ndepth * ntrack
    axes = ("depth", "track")
    angles, taps = taper.shape
    reach = (taps - 1) // 2
    slots = 2 * reach
    depth, traces, _ = primary.shape
    nloc = cell_of_group.shape[0]
    group = traces // nloc
    ncells = slowness_cells.shape[1]
    f32 = functools.partial(jax.ShapeDtypeStruct, dtype=jnp.float32)
    smem = pl.BlockSpec(memory_space=pltpu.SMEM)
    vmem = pl.BlockSpec(memory_space=pltpu.VMEM)
    hbm = pl.BlockSpec(memory_space=pl.ANY)

    cum, msg = pl.pallas_call(
        functools.partial(gather_kernel, nloc),
        out_shape=(f32((depth, LANES)), f32((SUBLANES, LANES))),
        in_specs=[smem, hbm],
        out_specs=(vmem, vmem),
        scratch_shapes=[pltpu.VMEM((nloc, depth, LANES), jnp.float32), pltpu.SemaphoreType.DMA((nloc,))],
        name="gather",
    )(cell_of_group, slowness_cells)
    msgs = lax.all_to_all(jnp.broadcast_to(msg[None], (ndev,) + msg.shape), axes, 0, 0)

    zb = 4
    block = pl.BlockSpec((zb, traces, angles), lambda i: (i, 0, 0))
    focused, sums, ids = pl.pallas_call(
        functools.partial(main_kernel, nloc, group, reach, ndepth, ntrack, zb),
        grid=(depth // zb,),
        out_shape=(
            f32((depth, traces)),
            f32((SUBLANES, LANES)),
            jax.ShapeDtypeStruct((ntrack, LANES), jnp.int32),
        ),
        in_specs=[
            whole(msgs.shape), whole(cum.shape), whole(taper.shape), whole((1, angles)),
            whole(observed.shape), block, block,
        ],
        out_specs=(whole((depth, traces)), whole((SUBLANES, LANES)), whole((ntrack, LANES))),
        scratch_shapes=[
            pltpu.VMEM((depth, LANES), jnp.float32),
            pltpu.SMEM((depth, LANES), jnp.float32),
            pltpu.VMEM((nloc, LANES), jnp.float32),
            pltpu.VMEM((4 * slots, angles), jnp.float32),
            pltpu.VMEM((depth, traces), jnp.float32),
            pltpu.VMEM((depth, traces), jnp.float32),
            pltpu.VMEM((nloc * slots, LANES), jnp.float32),
            pltpu.VMEM((nloc * slots, LANES), jnp.float32),
            pltpu.VMEM((nloc * slots, LANES), jnp.float32),
            pltpu.SemaphoreType.DMA,
        ],
        compiler_params=pltpu.CompilerParams(vmem_limit_bytes=40 * MIB),
        name="focus",
    )(msgs, cum, taper, secant.reshape(1, angles), observed, primary, quadrature)
    all_sums = lax.all_to_all(jnp.broadcast_to(sums[None], (ndev,) + sums.shape), axes, 0, 0)

    gradient = pl.pallas_call(
        functools.partial(scatter_kernel, nloc, ndepth, ntrack),
        out_shape=f32((depth, ncells)),
        in_specs=[vmem, smem],
        out_specs=vmem,
        compiler_params=pltpu.CompilerParams(vmem_limit_bytes=40 * MIB),
        name="scatter",
    )(all_sums, ids)
    return (focused, gradient)


def solution(mesh):
    in_specs = (
        P("depth", None),
        P("track"),
        P(),
        P(),
        P("depth", "track", None),
        P("depth", "track", None),
        P("depth", "track"),
    )
    out_specs = (P("depth", "track"), P("depth", None))
    return jax.shard_map(
        on_device, mesh=mesh, in_specs=in_specs, out_specs=out_specs, check_vma=False
    )
```

time: 363 us -> 57.8 us (0.16)
  other arithmetic: 158 us -> 0 us
  waiting for transfers between devices: 65.6 us -> 7.34 us
  local copies, waits for them, and re-layouts: 58.2 us -> 7.79 us
  matrix products: 34.4 us -> 0 us
  Pallas kernels: 0 us -> 24.3 us
  between operations: 15.1 us -> 0.67 us
  blocking collectives: 22.9 us -> 9.88 us
    reduce_sum x2 -> x0, other arithmetic: 67.1 us -> none  [the longest x1 66.9 us: on_device(): focused = jnp.sum(prim * cosine + quad * sine, axis=2)]
    mul x2 -> x0, other arithmetic: 66.8 us -> none  [on_device(): time_grad = OMEGA * resid[:, :, None] * (quad * cosine - prim * sine)]
    all_gather x2 -> x0, waiting for transfers between devices: 61.7 us -> none  [entering(): pieces = lax.all_gather(value, axis)]
    dot_general x2 -> x0, matrix products: 34.4 us -> none  [the longest x1 18.5 us: on_device(): jnp.einsum('zxa,ak->kzx', step_grad * secant, taper, precision=high)]
    rev x3 -> x0, local copies, waits for them, and re-layouts: 24.4 us -> none  [the longest x2 22.7 us: on_device(): deeper = jnp.flip(jnp.cumsum(jnp.flip(time_grad, 0), axis=0), 0)]
    pallas_call x0 -> x3, Pallas kernels: none -> 24.3 us  [the longest x1 16.7 us: on_device(): pl.pallas_call(functools.partial(main_kernel, nloc, group, reach, ndepth,...]
    unnamed x21 -> x9, local copies, waits for them, and re-layouts: 24.8 us -> 6.45 us
    all_gather x1 -> x0, blocking collectives: 14 us -> none  [on_device(): lax.all_gather(group_sums, 'track', axis=1, tiled=True)]
  transfers between devices with their start and end apart: 6 -> 1, of which waited for: 3 -> 1; matrix products, arithmetic and copies ran while one was open for 3% -> 1% of each run, Pallas kernels for 0% -> 0%
where the time goes in v1:
time: 57.8 us; the launch traced here: 57.3 us
  Pallas kernels  24.3 us (42%)
  blocking collectives  9.88 us (17%)
  local copies, waits for them, and re-layouts  7.79 us (13%)
  waiting for transfers between devices  7.34 us (13%)
  starting transfers between devices  7.3 us (13%)
  between operations  0.67 us (1%)
    pallas_call x1, Pallas kernels, on_device(): pl.pallas_call(functools.partial(main_kernel, nloc, group, reach, ndepth,...  16.7 us
    all_to_all x1, blocking collectives, on_device(): lax.all_to_all(jnp.broadcast_to(sums[None], (ndev,) + sums.shape), axes,...  9.88 us
    all_to_all x1, waiting for transfers between devices, on_device(): lax.all_to_all(jnp.broadcast_to(msg[None], (ndev,) + msg.shape), axes, 0, 0)  7.34 us
    all_to_all x1, starting transfers between devices, on_device(): lax.all_to_all(jnp.broadcast_to(msg[None], (ndev,) + msg.shape), axes, 0, 0)  7.3 us
    unnamed x9, local copies, waits for them, and re-layouts  6.45 us
    pallas_call x1, Pallas kernels, on_device(): pl.pallas_call(functools.partial(scatter_kernel, nloc, ndepth, ntrack), o...  3.96 us
    pallas_call x1, Pallas kernels, on_device(): pl.pallas_call(functools.partial(gather_kernel, nloc), out_shape=(f32((de...  3.61 us
    broadcast_in_dim x1, local copies, waits for them, and re-layouts, on_device(): jnp.broadcast_to(msg[None], (ndev,) + msg.shape)  1.34 us
  transfers between devices with their start and end apart: 1, of which 1 were waited for; matrix products, arithmetic and copies ran while one was open for 1% of the time, Pallas kernels for 0%

profile of v1, /device:TPU:0, one launch (start us, length us, event | category | flops | bytes accessed | tf_op | source)
XLA Modules:
  0.0 57.3 jit_solution(17283051718254276408)
XLA Ops:
  0.6 3.6 %gather.1 = (f32[32,128]{1,0:T(8,128)}, f32[8,128]{1,0:T(8,128)}) custom-call(s32[16]{0:T(128)} %cells_ref.1, f32[32,16384]{1,0:T(8,128)} %slow_ref.1), custom_call_target="tpu_custom_call" | custom-call | tf_op jit(solution)/shard_map/gather/pallas_call | solution.py:270
  4.2 1.3 %broadcast_in_dim.4 = f32[32,8,128]{2,1,0:T(8,128)} broadcast(f32[8,128]{1,0:T(8,128)} %get-tuple-element.7), dimensions={1,2} | broadcast | bytes 135168 | tf_op jit(solution)/shard_map/broadcast_in_dim | solution.py:278
  5.6 7.3 %all-to-all-start = ((f32[32,8,128]{2,1,0:T(8,128)}), f32[32,8,128]{2,1,0:T(8,128)S(1)}, u32[]{:S(2)}, u32[]{:S(2)}) async-start(f32[32,8,128]{2,1,0:T(8,128)} %broadcast_in_dim.4), calls=%async_computation | async-start | bytes 262144 | tf_op jit(solution)/shard_map/all_to_all | solution.py:278
  12.9 0.8 %copy.9.taper_ref = f32[256,9]{1,0:T(8,128)S(1)} copy(f32[256,9]{0,1:T(8,128)} %param.9) | data formatting | bytes 18432 | tf_op args[2]
  13.7 7.3 %all-to-all-done.m_ref = f32[32,8,128]{2,1,0:T(8,128)S(1)} async-done(((f32[32,8,128]{2,1,0:T(8,128)}), f32[32,8,128]{2,1,0:T(8,128)S(1)}, u32[]{:S(2)}, u32[]{:S(2)}) %all-to-all-start) | async-done | bytes 131104 | tf_op jit(solution)/shard_map/all_to_all | solution.py:278
  21.1 0.0 copy-start
  21.1 3.4 %copy-done = bf16[32,512,256]{2,1,0:T(8,128)(2,1)S(1)} copy-done((bf16[32,512,256]{2,1,0:T(8,128)(2,1)S(1)}, bf16[32,512,256]{2,1,0:T(8,128)(2,1)}, u32[]{:S(2)}) %copy-start) | copy-done | bytes 8388632
  24.4 0.0 copy-start.1
  24.4 0.8 %copy-done.1 = f32[32,512]{1,0:T(8,128)S(1)} copy-done((f32[32,512]{1,0:T(8,128)S(1)}, f32[32,512]{1,0:T(8,128)}, u32[]{:S(2)}) %copy-start.1) | copy-done | bytes 65560
  25.3 0.0 copy-start.2
  25.3 0.7 %copy-done.2 = f32[32,128]{1,0:T(8,128)S(1)} copy-done((f32[32,128]{1,0:T(8,128)S(1)}, f32[32,128]{1,0:T(8,128)}, u32[]{:S(2)}) %copy-start.2) | copy-done | bytes 16408
  26.0 0.0 copy-start.3
  26.0 0.7 %copy-done.3 = f32[256]{0:T(256)S(1)} copy-done((f32[256]{0:T(256)S(1)}, f32[256]{0:T(256)}, u32[]{:S(2)}) %copy-start.3) | copy-done | bytes 1048
  26.7 16.7 %focus.1 = (f32[32,512]{1,0:T(8,128)}, f32[8,128]{1,0:T(8,128)S(1)}, s32[8,128]{1,0:T(8,128)S(1)}) custom-call(f32[32,8,128]{2,1,0:T(8,128)S(1)} %all-to-all-done.m_ref, f32[32,128]{1,0:T(8,128)S(1)} %copy-done.2, f32[256,9]{1,0:T(8,128)S(1)} %copy.9.taper_ref, f32[1,256]{1,0:T(1,128)S(1)} %bitcast.1, f32[32,512]{1,0:T(8,128)S(1)} %copy-done.1, ...), custom_call_target="tpu_custom_call" | custom-call | tf_op jit(solution)/shard_map/focus/pallas_call | solution.py:282
  43.4 9.9 %all_to_all.10.m_ref = f32[32,8,128]{2,1,0:T(8,128)S(1)} all-to-all(f32[32,8,128]{2,1,0:T(8,128)S(1)} %broadcast_in_dim.5), channel_id=1, replica_groups=mesh['depth'=4,'track'=8] {'depth','track'}, dimensions={0} | all-to-all | bytes 262144 | tf_op jit(solution)/shard_map/all_to_all | solution.py:310
  53.3 4.0 %scatter.1 = f32[32,16384]{1,0:T(8,128)} custom-call(f32[32,8,128]{2,1,0:T(8,128)S(1)} %all_to_all.10.m_ref, s32[8,128]{1,0:T(8,128)S(1)} %get-tuple-element.11.ids_ref), custom_call_target="tpu_custom_call" | custom-call | tf_op jit(solution)/shard_map/scatter/pallas_call | solution.py:312
  (1 shorter events, 0.0 us)
Async XLA Ops:
  5.6 15.5 %all-to-all-start = ((f32[32,8,128]{2,1,0:T(8,128)}), f32[32,8,128]{2,1,0:T(8,128)S(1)}, u32[]{:S(2)}, u32[]{:S(2)}) async-start(f32[32,8,128]{2,1,0:T(8,128)} %broadcast_in_dim.4), calls=%async_computation | async-start | bytes 262144 | tf_op jit(solution)/shard_map/all_to_all | solution.py:278
  21.1 3.4 %copy-start = (bf16[32,512,256]{2,1,0:T(8,128)(2,1)S(1)}, bf16[32,512,256]{2,1,0:T(8,128)(2,1)}, u32[]{:S(2)}) copy-start(bf16[32,512,256]{2,1,0:T(8,128)(2,1)} %p_ref.1) | copy-start | bytes 25165828
  24.4 0.8 %copy-start.1 = (f32[32,512]{1,0:T(8,128)S(1)}, f32[32,512]{1,0:T(8,128)}, u32[]{:S(2)}) copy-start(f32[32,512]{1,0:T(8,128)} %obs_ref.1) | copy-start | bytes 196612
  25.3 0.7 %copy-start.2 = (f32[32,128]{1,0:T(8,128)S(1)}, f32[32,128]{1,0:T(8,128)}, u32[]{:S(2)}) copy-start(f32[32,128]{1,0:T(8,128)} %get-tuple-element.8.cum_ref) | copy-start | bytes 49156
  26.0 0.7 %copy-start.3 = (f32[256]{0:T(256)S(1)}, f32[256]{0:T(256)}, u32[]{:S(2)}) copy-start(f32[256]{0:T(256)} %param.10) | copy-start | bytes 3076

commit v2 on v0

v2 whole, which is shorter than its diff:
```python
import functools
import math

import jax
import jax.numpy as jnp
from jax import lax
from jax.experimental import pallas as pl
from jax.experimental.pallas import tpu as pltpu
from jax.sharding import PartitionSpec as P

OMEGA = 0.25
LANES = 128
SUBLANES = 8
MIB = 1024 * 1024
SINE = (4.442867755889893, -7.307443141937256, 3.594787359237671, -0.7843723297119141)
COSINE = (1.4142041206359863, -6.977642059326172, 5.71523904800415, -1.728348731994629)
HIGH = lax.Precision.HIGHEST
TURNS = OMEGA / (2 * math.pi)
NT = (((1,), (1,)), ((), ()))
TN = (((0,), (0,)), ((), ()))
NN = (((1,), (0,)), ((), ()))


def dot32(a, b, dims):
    return lax.dot_general(a, b, dims, precision=HIGH, preferred_element_type=jnp.float32)


def dot16(a, b, dims):
    return lax.dot_general(a, b, dims, preferred_element_type=jnp.float32)


def iota(shape, dim):
    return lax.broadcasted_iota(jnp.int32, shape, dim)


def cos_sin_turns(t):
    r = t - jnp.round(t)
    z = r * r
    s = r * (SINE[0] + z * (SINE[1] + z * (SINE[2] + z * SINE[3])))
    c = COSINE[0] + z * (COSINE[1] + z * (COSINE[2] + z * COSINE[3]))
    return 1.0 - s * s, s * c


def split(x):
    hi = x.astype(jnp.bfloat16)
    return hi, (x - hi.astype(jnp.float32)).astype(jnp.bfloat16)


def pack(rows, width):
    lane = iota((SUBLANES, LANES), 1)
    packed = rows[:SUBLANES]
    for part in range(1, rows.shape[0] // SUBLANES):
        piece = pltpu.roll(rows[part * SUBLANES : (part + 1) * SUBLANES], part * width, 1)
        packed = jnp.where(lane // width == part, piece, packed)
    return packed


def unpack(packed, parts):
    width = LANES // parts
    return jnp.concatenate([packed] + [pltpu.roll(packed, LANES - k * width, 1) for k in range(1, parts)], axis=0)


def pairs(count, first):
    swaps = [(i, i + 1) for i in range(first, count - 1, 2)]
    return swaps + [(j, i) for i, j in swaps]


def gather_kernel(nloc, ntrack, cells_ref, even_ref, odd_ref, slow_ref, cum_ref, msg_ref, buf, sems):
    depth = slow_ref.shape[0]
    t = lax.axis_index("track")
    even = lax.rem(t, 2) == 0
    left = jnp.where(even, odd_ref[nloc - 1], even_ref[nloc - 1])
    right = jnp.where(even, even_ref[0], odd_ref[0])
    cells = [left] + [cells_ref[g] for g in range(nloc)] + [right]

    def copy(j):
        start = pl.multiple_of((cells[j] // LANES) * LANES, LANES)
        return pltpu.make_async_copy(slow_ref.at[:, pl.ds(start, LANES)], buf.at[j], sems.at[j])

    for j in range(nloc + 2):
        copy(j).start()
    lane = iota((depth, LANES), 1)
    slow = jnp.zeros((depth, LANES), jnp.float32)
    for j in range(nloc + 2):
        copy(j).wait()
        shift = lax.rem(j + LANES - lax.rem(cells[j], LANES), LANES)
        slow = jnp.where(lane == j, pltpu.roll(buf[j], shift, 1), slow)
    first = (t == 0).astype(jnp.int32)
    last = (t < ntrack - 1).astype(jnp.int32)
    slow = jnp.where((lane >= first) & (lane < nloc + 1 + last), slow, 0.0)
    lower = (iota((depth, depth), 0) >= iota((depth, depth), 1)).astype(jnp.float32)
    cum = dot32(lower, slow, NN)
    cum_ref[...] = cum
    msg_ref[...] = jnp.broadcast_to(cum[depth - 1 :], msg_ref.shape)


def weight_rows(taper_ref, sec_ref, reach):
    taps, slots = taper_ref.shape[0], 2 * reach
    slot = iota((2 * slots, taps), 0)
    k = iota((2 * slots, taps), 1)
    i = lax.rem(slot, slots)
    near = ((i < reach) & (k < reach - i)) | ((i >= reach) & (k >= 2 * reach - (i - reach)))
    near = near.astype(jnp.float32)
    mask = jnp.where(slot < slots, 1.0 - near, near)
    weights = dot32(mask, taper_ref[...], NN) * sec_ref[...]
    return weights[:slots], weights[slots:]


def fetches(pairs, sems):
    copies = [pltpu.make_async_copy(source, target, sems.at[k]) for k, (source, target) in enumerate(pairs)]
    for copy in copies:
        copy.start()
    return copies


def focus_kernel(
    nloc, group, reach, count,
    *refs,
):
    totals = refs[: count - 1]
    (
        cells_ref, cum_hbm, taper_hbm, sec_hbm, obs_hbm, p_ref, q_ref,
        foc_ref, msg_ref,
        cum_ref, taper_ref, sec_ref, obs_ref, c_vmem, c_smem, b_ref, cent, edge_f, edge_o, edge_n,
        sem, small,
    ) = refs[count - 1 :]
    depth, traces = obs_ref.shape
    fetch = fetches(
        ((cum_hbm, cum_ref), (taper_hbm, taper_ref), (sec_hbm, sec_ref), (obs_hbm, obs_ref)), small
    )
    d = lax.axis_index("depth")
    slots = 2 * reach
    parts = depth // SUBLANES
    width = LANES // parts
    above = jnp.zeros((1, LANES), jnp.float32)
    for k, ref in enumerate(totals):
        above += ((d ^ (k + 1)) < d).astype(jnp.float32) * ref[0:1, :]
    for copy in fetch:
        copy.wait()
    c_ext = cum_ref[...] + above
    c_vmem[...] = c_ext
    copy = pltpu.make_async_copy(c_vmem, c_smem, sem)
    copy.start()
    own_w, near_w = weight_rows(taper_ref, sec_ref, reach)
    own_t, near_t = own_w * TURNS, near_w * TURNS
    all_w = (own_w + near_w)[0:1, :]
    all_t = all_w * TURNS
    upper = iota((slots, 1), 0) < reach
    lane_z = iota((depth, LANES), 1)

    def waves(g, carry):
        column = jnp.sum(jnp.where(lane_z == g + 1, c_ext, 0.0), axis=1, keepdims=True)
        c, s = cos_sin_turns(column * all_t)
        b_ref[g, 0] = jnp.concatenate(split(c) + split(-all_w * s), axis=0)
        b_ref[g, 1] = jnp.concatenate(split(s) + split(all_w * c), axis=0)
        return carry

    lax.fori_loop(0, nloc, waves, 0, unroll=4)
    col = lax.rem(iota((group, LANES), 1), depth)
    lane = iota((slots, LANES), 1)

    def one(g, carry):
        home = pl.ds(pl.multiple_of(g * group, group), group)
        out = jnp.zeros((group, LANES), jnp.float32)
        sums = [jnp.zeros((slots, LANES), jnp.float32)] * 3
        for first in range(0, depth, SUBLANES):
            at = pl.ds(first, SUBLANES)
            both = dot16(p_ref[at, home].reshape(SUBLANES * group, -1), b_ref[g, 0], NT)
            both += dot16(q_ref[at, home].reshape(SUBLANES * group, -1), b_ref[g, 1], NT)
            for z in range(first, first + SUBLANES):
                near = jnp.where(upper, c_smem[z, g], c_smem[z, g + 2])
                c, s = cos_sin_turns(own_t * c_smem[z, g + 1] + near_t * near)

                def rows(ref):
                    mine = ref[z, home]
                    low, high = mine[: 2 * SUBLANES].astype(jnp.float32), mine[group - 2 * SUBLANES :].astype(jnp.float32)
                    return jnp.where(upper, low[:slots], high[2 * SUBLANES - slots :])

                p, q = rows(p_ref), rows(q_ref)
                f = p * c + q * s
                dd = q * c - p * s
                values = (f, dd * own_w, dd * near_w)
                sums = [
                    jnp.where(lane == z, jnp.sum(value, axis=1, keepdims=True), old) for value, old in zip(values, sums)
                ]
            for z in range(first, first + SUBLANES):
                k = (z - first) * group
                out = jnp.where(col == z, both[k : k + group], out)
        cent[home, :] = out
        at = pl.ds(pl.multiple_of(g * slots, slots), slots)
        for ref, value in zip((edge_f, edge_o, edge_n), sums):
            ref[at, :] = value
        return carry

    copy.wait()
    lax.fori_loop(0, nloc, one, 0)

    gather = (iota((depth, LANES), 1) == iota((depth, LANES), 0)).astype(jnp.float32)
    count = nloc * slots
    e, x = iota((count, traces), 0), iota((count, traces), 1)
    i = lax.rem(e, slots)
    spread = (x == (e // slots) * group + jnp.where(i < reach, i, group - slots + i)).astype(jnp.float32)
    edge = jnp.concatenate([dot32(gather, ref[...], NT) for ref in (edge_f, edge_o, edge_n)], axis=0)
    edge = dot32(edge, spread, NN)
    r = lax.rem(iota((depth, traces), 1), group)
    is_edge = (r < reach) | (r >= group - reach)
    cent_t = jnp.transpose(cent[...])
    cent_f = cent_t[0:depth] + cent_t[depth : 2 * depth]
    cent_e = cent_t[2 * depth : 3 * depth] + cent_t[3 * depth :]
    focused = jnp.where(is_edge, edge[:depth], cent_f)
    foc_ref[...] = focused
    resid = OMEGA * (focused - obs_ref[...])
    a = resid * jnp.where(is_edge, edge[depth : 2 * depth], cent_e)
    b = resid * edge[2 * depth :]
    x, lane_g = iota((traces, LANES), 0), iota((traces, LANES), 1)
    r, g = lax.rem(x, group), x // group
    to_own = (lane_g == g + 1).astype(jnp.float32)
    to_near = ((r < reach) & (lane_g == g)) | ((r >= group - reach) & (lane_g == g + 2))
    sums = dot32(a, to_own, NN) + dot32(b, to_near.astype(jnp.float32), NN)
    later = (iota((depth, depth), 1) >= iota((depth, depth), 0)).astype(jnp.float32)
    tile = pack(dot32(later, sums, NN), width)
    row, lane8 = iota((SUBLANES, LANES), 0), iota((SUBLANES, LANES), 1)
    for g in range(nloc):
        at = (row == g % SUBLANES) & (lane8 == nloc + 2 + g // SUBLANES)
        tile = jnp.where(at, cells_ref[g].astype(jnp.float32), tile)
    msg_ref[...] = tile


def scatter_kernel(nloc, ndepth, ntrack, m_ref, out_ref, ids_vmem, ids_ref, sem):
    depth = out_ref.shape[0]
    d = lax.axis_index("depth")
    parts = depth // SUBLANES
    lane = iota((depth, LANES), 1)
    for s in range(ntrack):
        at = SUBLANES * s
        ids_vmem[at : at + SUBLANES, :] = m_ref[d * ntrack + s].astype(jnp.int32)
    copy = pltpu.make_async_copy(ids_vmem, ids_ref, sem)
    copy.start()
    out_ref[...] = jnp.zeros(out_ref.shape, jnp.float32)
    copy.wait()

    def cell_of(s, g):
        return ids_ref[SUBLANES * s + g % SUBLANES, nloc + 2 + g // SUBLANES]

    def segment(s, carry):
        below = jnp.zeros((1, LANES), jnp.float32)
        for e in range(1, ndepth):
            below += (e > d).astype(jnp.float32) * m_ref[e * ntrack + s, 0:1, :]
        sums = unpack(m_ref[d * ntrack + s], parts) + below
        for j in range(nloc + 2):
            if j == 0:
                cell, on = cell_of(jnp.maximum(s - 1, 0), nloc - 1), s > 0
            elif j == nloc + 1:
                cell, on = cell_of(jnp.minimum(s + 1, ntrack - 1), 0), s < ntrack - 1
            else:
                cell, on = cell_of(s, j - 1), True
            at = lax.rem(cell, LANES)
            start = pl.multiple_of((cell // LANES) * LANES, LANES)
            moved = pltpu.roll(sums, lax.rem(at + LANES - j, LANES), 1)
            hit = lane == jnp.where(on, at, -1)
            out_ref[:, pl.ds(start, LANES)] += jnp.where(hit, moved, 0.0)
        return carry

    lax.fori_loop(0, ntrack, segment, 0)


def whole(shape):
    return pl.BlockSpec(shape, lambda *_: (0,) * len(shape))


def on_device(slowness_cells, cell_of_group, taper, secant, primary, quadrature, observed):
    ndepth, ntrack = lax.axis_size("depth"), lax.axis_size("track")
    ndev = ndepth * ntrack
    axes = ("depth", "track")
    angles, taps = taper.shape
    reach = (taps - 1) // 2
    slots = 2 * reach
    depth, traces, _ = primary.shape
    nloc = cell_of_group.shape[0]
    group = traces // nloc
    ncells = slowness_cells.shape[1]
    f32 = functools.partial(jax.ShapeDtypeStruct, dtype=jnp.float32)
    smem = pl.BlockSpec(memory_space=pltpu.SMEM)
    vmem = pl.BlockSpec(memory_space=pltpu.VMEM)
    hbm = pl.BlockSpec(memory_space=pl.ANY)

    even = lax.ppermute(cell_of_group, "track", pairs(ntrack, 0))
    odd = lax.ppermute(cell_of_group, "track", pairs(ntrack, 1))
    cum, total = pl.pallas_call(
        functools.partial(gather_kernel, nloc, ntrack),
        out_shape=(f32((depth, LANES)), f32((SUBLANES, LANES))),
        in_specs=[smem, smem, smem, hbm],
        out_specs=(vmem, vmem),
        scratch_shapes=[
            pltpu.VMEM((nloc + 2, depth, LANES), jnp.float32),
            pltpu.SemaphoreType.DMA((nloc + 2,)),
        ],
        compiler_params=pltpu.CompilerParams(vmem_limit_bytes=4 * MIB),
        cost_estimate=pl.CostEstimate(flops=10**11, bytes_accessed=10**7, transcendentals=0),
        name="gather",
    )(cell_of_group, even, odd, slowness_cells)
    totals = [
        lax.ppermute(total, "depth", [(i, i ^ k) for i in range(ndepth)]) for k in range(1, ndepth)
    ]
    focused, sums = pl.pallas_call(
        functools.partial(focus_kernel, nloc, group, reach, ndepth),
        out_shape=(f32((depth, traces)), f32((SUBLANES, LANES))),
        in_specs=[vmem] * (ndepth - 1) + [smem] + [hbm] * 4 + [vmem] * 2,
        out_specs=(vmem, vmem),
        scratch_shapes=[
            pltpu.VMEM((depth, LANES), jnp.float32),
            pltpu.VMEM((taps, angles), jnp.float32),
            pltpu.VMEM((1, angles), jnp.float32),
            pltpu.VMEM((depth, traces), jnp.float32),
            pltpu.VMEM((depth, LANES), jnp.float32),
            pltpu.SMEM((depth, LANES), jnp.float32),
            pltpu.VMEM((nloc, 2, 4 * depth, angles), jnp.bfloat16),
            pltpu.VMEM((traces, LANES), jnp.float32),
            pltpu.VMEM((nloc * slots, LANES), jnp.float32),
            pltpu.VMEM((nloc * slots, LANES), jnp.float32),
            pltpu.VMEM((nloc * slots, LANES), jnp.float32),
            pltpu.SemaphoreType.DMA,
            pltpu.SemaphoreType.DMA((4,)),
        ],
        compiler_params=pltpu.CompilerParams(vmem_limit_bytes=20 * MIB),
        name="focus",
    )(*totals, cell_of_group, cum, taper.T, secant.reshape(1, angles), observed, primary, quadrature)
    all_sums = lax.all_to_all(jnp.broadcast_to(sums[None], (ndev,) + sums.shape), axes, 0, 0)

    gradient = pl.pallas_call(
        functools.partial(scatter_kernel, nloc, ndepth, ntrack),
        out_shape=f32((depth, ncells)),
        in_specs=[vmem],
        out_specs=vmem,
        scratch_shapes=[
            pltpu.VMEM((SUBLANES * ntrack, LANES), jnp.int32),
            pltpu.SMEM((SUBLANES * ntrack, LANES), jnp.int32),
            pltpu.SemaphoreType.DMA,
        ],
        compiler_params=pltpu.CompilerParams(vmem_limit_bytes=60 * MIB),
        name="scatter",
    )(all_sums)
    return (focused, gradient)


def solution(mesh):
    in_specs = (
        P("depth", None),
        P("track"),
        P(),
        P(),
        P("depth", "track", None),
        P("depth", "track", None),
        P("depth", "track"),
    )
    out_specs = (P("depth", "track"), P("depth", None))
    return jax.shard_map(
        on_device, mesh=mesh, in_specs=in_specs, out_specs=out_specs, check_vma=False
    )
```

time: 363 us -> 50.8 us (0.14)
  other arithmetic: 158 us -> 0 us
  waiting for transfers between devices: 65.6 us -> 4.02 us
  local copies, waits for them, and re-layouts: 58.2 us -> 2.28 us
  matrix products: 34.4 us -> 0 us
  Pallas kernels: 0 us -> 21 us
  between operations: 15.1 us -> 0.74 us
  blocking collectives: 22.9 us -> 13.5 us
    reduce_sum x2 -> x0, other arithmetic: 67.1 us -> none  [the longest x1 66.9 us: on_device(): focused = jnp.sum(prim * cosine + quad * sine, axis=2)]
    mul x2 -> x0, other arithmetic: 66.8 us -> none  [on_device(): time_grad = OMEGA * resid[:, :, None] * (quad * cosine - prim * sine)]
    all_gather x2 -> x0, waiting for transfers between devices: 61.7 us -> none  [entering(): pieces = lax.all_gather(value, axis)]
    dot_general x2 -> x0, matrix products: 34.4 us -> none  [the longest x1 18.5 us: on_device(): jnp.einsum('zxa,ak->kzx', step_grad * secant, taper, precision=high)]
    rev x3 -> x0, local copies, waits for them, and re-layouts: 24.4 us -> none  [the longest x2 22.7 us: on_device(): deeper = jnp.flip(jnp.cumsum(jnp.flip(time_grad, 0), axis=0), 0)]
    unnamed x21 -> x16, local copies, waits for them, and re-layouts: 24.8 us -> 2.27 us
    pallas_call x0 -> x3, Pallas kernels: none -> 21 us  [the longest x1 13.3 us: on_device(): pl.pallas_call(functools.partial(focus_kernel, nloc, group, reach, ndepth...]
    all_gather x1 -> x0, blocking collectives: 14 us -> none  [on_device(): lax.all_gather(group_sums, 'track', axis=1, tiled=True)]
  transfers between devices with their start and end apart: 6 -> 5, of which waited for: 3 -> 4; matrix products, arithmetic and copies ran while one was open for 3% -> 0% of each run, Pallas kernels for 0% -> 0%
where the time goes in v2:
time: 50.8 us; the launch traced here: 50.6 us
  Pallas kernels  21 us (41%)
  blocking collectives  13.5 us (27%)
  starting transfers between devices  9.06 us (18%)
  waiting for transfers between devices  4.02 us (8%)
  local copies, waits for them, and re-layouts  2.28 us (4%)
  between operations  0.74 us (1%)
    all_to_all x1, blocking collectives, on_device(): lax.all_to_all(jnp.broadcast_to(sums[None], (ndev,) + sums.shape), axes,...  13.5 us
    pallas_call x1, Pallas kernels, on_device(): pl.pallas_call(functools.partial(focus_kernel, nloc, group, reach, ndepth...  13.3 us
    pallas_call x1, Pallas kernels, on_device(): pl.pallas_call(functools.partial(scatter_kernel, nloc, ndepth, ntrack), o...  5.31 us
    ppermute x1, starting transfers between devices, on_device(): even = lax.ppermute(cell_of_group, 'track', pairs(ntrack, 0))  4.71 us
    ppermute x3, starting transfers between devices, on_device(): lax.ppermute(total, 'depth', [(i, i ^ k) for i in range(ndepth)])  3.55 us
    ppermute x3, waiting for transfers between devices, on_device(): lax.ppermute(total, 'depth', [(i, i ^ k) for i in range(ndepth)])  3.07 us
    pallas_call x1, Pallas kernels, on_device(): pl.pallas_call(functools.partial(gather_kernel, nloc, ntrack), out_shape=...  2.4 us
    unnamed x16, local copies, waits for them, and re-layouts  2.27 us
  transfers between devices with their start and end apart: 5, of which 4 were waited for; matrix products, arithmetic and copies ran while one was open for 0% of the time, Pallas kernels for 0%

profile of v2, /device:TPU:0, one launch (start us, length us, event | category | flops | bytes accessed | tf_op | source)
XLA Modules:
  0.0 50.6 jit_solution(12717565563398606546)
XLA Ops:
  0.6 0.0 copy-start.2
  0.6 0.0 copy-start.1
  0.7 0.0 copy-start
  0.7 0.0 copy-start.4
  0.7 0.0 copy-start.3
  0.7 0.8 %collective-permute-start.1 = (s32[16]{0:T(128)}, s32[16]{0:T(128)S(1)}, u32[]{:S(2)}, u32[]{:S(2)}) collective-permute-start(s32[16]{0:T(128)} %refs_3_.1), channel_id=1, source_target_pairs={{1,2},{3,4},{5,6},{2,1},{4,3},{6,5},{9,10},{11,12},{13,14},{10,9},... | collective-permute-start | bytes 200 | tf_op jit(solution)/shard_map/ppermute | solution.py:288
  1.5 4.7 %collective-permute-start = (s32[16]{0:T(128)}, s32[16]{0:T(128)S(1)}, u32[]{:S(2)}, u32[]{:S(2)}) collective-permute-start(s32[16]{0:T(128)} %refs_3_.1), channel_id=1, source_target_pairs={{0,1},{2,3},{4,5},{6,7},{1,0},{3,2},{5,4},{7,6},{8,9},{10,11},{12,... | collective-permute-start | bytes 200 | tf_op jit(solution)/shard_map/ppermute | solution.py:287
  6.2 0.0 collective-permute-done.1.odd_ref
  6.2 0.9 %collective-permute-done.even_ref = s32[16]{0:T(128)S(1)} collective-permute-done((s32[16]{0:T(128)}, s32[16]{0:T(128)S(1)}, u32[]{:S(2)}, u32[]{:S(2)}) %collective-permute-start) | collective-permute-done | bytes 96 | tf_op jit(solution)/shard_map/ppermute | solution.py:287
  7.2 0.0 copy-start.5
  7.2 0.7 %copy-done.5 = s32[16]{0:T(128)S(1)} copy-done((s32[16]{0:T(128)S(1)}, s32[16]{0:T(128)}, u32[]{:S(2)}) %copy-start.5) | copy-done | bytes 88
  7.8 0.0 copy-start.7
  7.8 1.6 %copy-done.7 = f32[32,16384]{1,0:T(8,128)S(1)} copy-done((f32[32,16384]{1,0:T(8,128)S(1)}, f32[32,16384]{1,0:T(8,128)}, u32[]{:S(2)}) %copy-start.7) | copy-done | bytes 2097176
  9.4 0.0 copy-start.6
  9.4 2.4 %gather.1 = (f32[32,128]{1,0:T(8,128)S(1)}, f32[8,128]{1,0:T(8,128)S(1)}) custom-call(s32[16]{0:T(128)S(1)} %copy-done.5, s32[16]{0:T(128)S(1)} %collective-permute-done.even_ref, s32[16]{0:T(128)S(1)} %collective-permute-done.1.odd_ref, f32[32,16384]{1,0:T(8,128)S(1)} %copy-done.7), custom_call_target="tpu_custom_call" | custom-call | flops 99999997952 | bytes 10000000 | tf_op jit(solution)/shard_map/gather/pallas_call | solution.py:289
  11.8 2.5 %collective-permute-start.4 = (f32[8,128]{1,0:T(8,128)S(1)}, f32[8,128]{1,0:T(8,128)S(1)}, u32[]{:S(2)}, u32[]{:S(2)}) collective-permute-start(f32[8,128]{1,0:T(8,128)S(1)} %get-tuple-element.6), channel_id=1, source_target_pairs={{0,24},{8,16},{16,8},{24,0},{1,25},{9,17},{17,9},{25,1},{2,26},{10... | collective-permute-start | bytes 12296 | tf_op jit(solution)/shard_map/ppermute | solution.py:303
  14.3 0.5 collective-permute-start.3
  14.8 0.5 %collective-permute-start.2 = (f32[8,128]{1,0:T(8,128)S(1)}, f32[8,128]{1,0:T(8,128)S(1)}, u32[]{:S(2)}, u32[]{:S(2)}) collective-permute-start(f32[8,128]{1,0:T(8,128)S(1)} %get-tuple-element.6), channel_id=1, source_target_pairs={{0,8},{8,0},{16,24},{24,16},{1,9},{9,1},{17,25},{25,17},{2,10},{10... | collective-permute-start | bytes 12296 | tf_op jit(solution)/shard_map/ppermute | solution.py:303
  15.4 1.0 %collective-permute-done.4.refs_2_ = f32[8,128]{1,0:T(8,128)S(1)} collective-permute-done((f32[8,128]{1,0:T(8,128)S(1)}, f32[8,128]{1,0:T(8,128)S(1)}, u32[]{:S(2)}, u32[]{:S(2)}) %collective-permute-start.4) | collective-permute-done | bytes 4128 | tf_op jit(solution)/shard_map/ppermute | solution.py:303
  16.4 1.5 %collective-permute-done.3.refs_1_ = f32[8,128]{1,0:T(8,128)S(1)} collective-permute-done((f32[8,128]{1,0:T(8,128)S(1)}, f32[8,128]{1,0:T(8,128)S(1)}, u32[]{:S(2)}, u32[]{:S(2)}) %collective-permute-start.3) | collective-permute-done | bytes 4128 | tf_op jit(solution)/shard_map/ppermute | solution.py:303
  17.9 0.5 collective-permute-done.2.refs_0_
  18.4 0.0 copy-done.2
  18.4 0.0 copy-done.1
  18.4 0.0 copy-done
  18.4 0.0 copy-done.4
  18.5 0.0 copy-done.3
  18.5 0.0 copy-done.6
  18.5 13.3 %focus.1 = (f32[32,512]{1,0:T(8,128)}, f32[8,128]{1,0:T(8,128)S(1)}) custom-call(f32[8,128]{1,0:T(8,128)S(1)} %collective-permute-done.2.refs_0_, f32[8,128]{1,0:T(8,128)S(1)} %collective-permute-done.3.refs_1_, f32[8,128]{1,0:T(8,128)S(1)} %collective-permute-done.4.refs_2_, s32[16]{0:T(128)S(1)} %copy-done.6, f32[32,128]{1,0:T(8,128)S(1)} %get-tuple-element.7.refs_4_, ...), custom_call_target="tpu_custom_call" | custom-call | tf_op jit(solution)/shard_map/focus/pallas_call | solution.py:305
  31.8 13.5 %all_to_all.5.m_ref = f32[32,8,128]{2,1,0:T(8,128)} all-to-all(f32[32,8,128]{2,1,0:T(8,128)S(1)} %broadcast_in_dim.2), channel_id=1, replica_groups=mesh['depth'=4,'track'=8] {'depth','track'}, dimensions={0} | all-to-all | bytes 262144 | tf_op jit(solution)/shard_map/all_to_all | solution.py:328
  45.3 5.3 %scatter.1 = f32[32,16384]{1,0:T(8,128)} custom-call(f32[32,8,128]{2,1,0:T(8,128)} %all_to_all.5.m_ref), custom_call_target="tpu_custom_call" | custom-call | tf_op jit(solution)/shard_map/scatter/pallas_call | solution.py:330
  (1 shorter events, 0.0 us)
Async XLA Ops:
  0.6 17.8 %copy-start.2 = (f32[32,512]{1,0:T(8,128)S(1)}, f32[32,512]{1,0:T(8,128)}, u32[]{:S(2)}) copy-start(f32[32,512]{1,0:T(8,128)} %refs_7_.1) | copy-start | bytes 196612
  0.6 17.8 %copy-start.1 = (bf16[32,512,256]{2,1,0:T(8,128)(2,1)S(1)}, bf16[32,512,256]{2,1,0:T(8,128)(2,1)}, u32[]{:S(2)}) copy-start(bf16[32,512,256]{2,1,0:T(8,128)(2,1)} %refs_9_.1) | copy-start | bytes 25165828
  0.7 17.8 %copy-start = (bf16[32,512,256]{2,1,0:T(8,128)(2,1)S(1)}, bf16[32,512,256]{2,1,0:T(8,128)(2,1)}, u32[]{:S(2)}) copy-start(bf16[32,512,256]{2,1,0:T(8,128)(2,1)} %refs_8_.1) | copy-start | bytes 25165828
  0.7 17.8 %copy-start.4 = (f32[256]{0:T(256)S(1)}, f32[256]{0:T(256)}, u32[]{:S(2)}) copy-start(f32[256]{0:T(256)} %param.10) | copy-start | bytes 3076
  0.7 17.8 %copy-start.3 = (f32[256,9]{0,1:T(8,128)S(1)}, f32[256,9]{0,1:T(8,128)}, u32[]{:S(2)}) copy-start(f32[256,9]{0,1:T(8,128)} %param.9) | copy-start | bytes 27652
  0.7 5.5 %collective-permute-start.1 = (s32[16]{0:T(128)}, s32[16]{0:T(128)S(1)}, u32[]{:S(2)}, u32[]{:S(2)}) collective-permute-start(s32[16]{0:T(128)} %refs_3_.1), channel_id=1, source_target_pairs={{1,2},{3,4},{5,6},{2,1},{4,3},{6,5},{9,10},{11,12},{13,14},{10,9},... | collective-permute-start | bytes 200 | tf_op jit(solution)/shard_map/ppermute | solution.py:288
  1.5 5.7 %collective-permute-start = (s32[16]{0:T(128)}, s32[16]{0:T(128)S(1)}, u32[]{:S(2)}, u32[]{:S(2)}) collective-permute-start(s32[16]{0:T(128)} %refs_3_.1), channel_id=1, source_target_pairs={{0,1},{2,3},{4,5},{6,7},{1,0},{3,2},{5,4},{7,6},{8,9},{10,11},{12,... | collective-permute-start | bytes 200 | tf_op jit(solution)/shard_map/ppermute | solution.py:287
  7.2 0.7 %copy-start.5 = (s32[16]{0:T(128)S(1)}, s32[16]{0:T(128)}, u32[]{:S(2)}) copy-start(s32[16]{0:T(128)} %refs_3_.1) | copy-start | bytes 196
  7.8 1.6 %copy-start.7 = (f32[32,16384]{1,0:T(8,128)S(1)}, f32[32,16384]{1,0:T(8,128)}, u32[]{:S(2)}) copy-start(f32[32,16384]{1,0:T(8,128)} %slow_ref.1) | copy-start | bytes 6291460
  9.4 9.1 %copy-start.6 = (s32[16]{0:T(128)S(1)}, s32[16]{0:T(128)}, u32[]{:S(2)}) copy-start(s32[16]{0:T(128)} %refs_3_.1) | copy-start | bytes 196
  11.8 4.6 %collective-permute-start.4 = (f32[8,128]{1,0:T(8,128)S(1)}, f32[8,128]{1,0:T(8,128)S(1)}, u32[]{:S(2)}, u32[]{:S(2)}) collective-permute-start(f32[8,128]{1,0:T(8,128)S(1)} %get-tuple-element.6), channel_id=1, source_target_pairs={{0,24},{8,16},{16,8},{24,0},{1,25},{9,17},{17,9},{25,1},{2,26},{10... | collective-permute-start | bytes 12296 | tf_op jit(solution)/shard_map/ppermute | solution.py:303
  14.3 3.6 %collective-permute-start.3 = (f32[8,128]{1,0:T(8,128)S(1)}, f32[8,128]{1,0:T(8,128)S(1)}, u32[]{:S(2)}, u32[]{:S(2)}) collective-permute-start(f32[8,128]{1,0:T(8,128)S(1)} %get-tuple-element.6), channel_id=1, source_target_pairs={{0,16},{8,24},{16,0},{24,8},{1,17},{9,25},{17,1},{25,9},{2,18},{10... | collective-permute-start | bytes 12296 | tf_op jit(solution)/shard_map/ppermute | solution.py:303
  14.8 3.6 %collective-permute-start.2 = (f32[8,128]{1,0:T(8,128)S(1)}, f32[8,128]{1,0:T(8,128)S(1)}, u32[]{:S(2)}, u32[]{:S(2)}) collective-permute-start(f32[8,128]{1,0:T(8,128)S(1)} %get-tuple-element.6), channel_id=1, source_target_pairs={{0,8},{8,0},{16,24},{24,16},{1,9},{9,1},{17,25},{25,17},{2,10},{10... | collective-permute-start | bytes 12296 | tf_op jit(solution)/shard_map/ppermute | solution.py:303

commit v3 on v2

--- a/solution.py
+++ b/solution.py
@@ -135,12 +135,13 @@
     above = jnp.zeros((1, LANES), jnp.float32)
     for k, ref in enumerate(totals):
         above += ((d ^ (k + 1)) < d).astype(jnp.float32) * ref[0:1, :]
-    for copy in fetch:
-        copy.wait()
+    fetch[0].wait()
     c_ext = cum_ref[...] + above
     c_vmem[...] = c_ext
     copy = pltpu.make_async_copy(c_vmem, c_smem, sem)
     copy.start()
+    fetch[1].wait()
+    fetch[2].wait()
     own_w, near_w = weight_rows(taper_ref, sec_ref, reach)
     own_t, near_t = own_w * TURNS, near_w * TURNS
     all_w = (own_w + near_w)[0:1, :]
@@ -193,7 +194,7 @@
         return carry
 
     copy.wait()
-    lax.fori_loop(0, nloc, one, 0)
+    lax.fori_loop(0, nloc, one, 0, unroll=2)
 
     gather = (iota((depth, LANES), 1) == iota((depth, LANES), 0)).astype(jnp.float32)
     count = nloc * slots
@@ -209,6 +210,7 @@
     cent_e = cent_t[2 * depth : 3 * depth] + cent_t[3 * depth :]
     focused = jnp.where(is_edge, edge[:depth], cent_f)
     foc_ref[...] = focused
+    fetch[3].wait()
     resid = OMEGA * (focused - obs_ref[...])
     a = resid * jnp.where(is_edge, edge[depth : 2 * depth], cent_e)
     b = resid * edge[2 * depth :]
@@ -226,8 +228,8 @@
     msg_ref[...] = tile
 
 
-def scatter_kernel(nloc, ndepth, ntrack, m_ref, out_ref, ids_vmem, ids_ref, sem):
-    depth = out_ref.shape[0]
+def scatter_kernel(nloc, ndepth, ntrack, m_ref, out_hbm, acc, ids_vmem, ids_ref, sem, out_sems):
+    depth = acc.shape[1]
     d = lax.axis_index("depth")
     parts = depth // SUBLANES
     lane = iota((depth, LANES), 1)
@@ -236,36 +238,45 @@
         ids_vmem[at : at + SUBLANES, :] = m_ref[d * ntrack + s].astype(jnp.int32)
     copy = pltpu.make_async_copy(ids_vmem, ids_ref, sem)
     copy.start()
-    out_ref[...] = jnp.zeros(out_ref.shape, jnp.float32)
+    acc[...] = jnp.zeros(acc.shape, jnp.float32)
     copy.wait()
 
     def cell_of(s, g):
         return ids_ref[SUBLANES * s + g % SUBLANES, nloc + 2 + g // SUBLANES]
 
-    def segment(s, carry):
+    def sums_of(s):
         below = jnp.zeros((1, LANES), jnp.float32)
         for e in range(1, ndepth):
             below += (e > d).astype(jnp.float32) * m_ref[e * ntrack + s, 0:1, :]
-        sums = unpack(m_ref[d * ntrack + s], parts) + below
+        return unpack(m_ref[d * ntrack + s], parts) + below
+
+    def two(pair, carry):
+        segments = (2 * pair, 2 * pair + 1)
+        sums = [sums_of(s) for s in segments]
         for j in range(nloc + 2):
-            if j == 0:
-                cell, on = cell_of(jnp.maximum(s - 1, 0), nloc - 1), s > 0
-            elif j == nloc + 1:
-                cell, on = cell_of(jnp.minimum(s + 1, ntrack - 1), 0), s < ntrack - 1
-            else:
-                cell, on = cell_of(s, j - 1), True
-            at = lax.rem(cell, LANES)
-            start = pl.multiple_of((cell // LANES) * LANES, LANES)
-            moved = pltpu.roll(sums, lax.rem(at + LANES - j, LANES), 1)
-            hit = lane == jnp.where(on, at, -1)
-            out_ref[:, pl.ds(start, LANES)] += jnp.where(hit, moved, 0.0)
+            for k, s in enumerate(segments):
+                if j == 0:
+                    cell, on = cell_of(jnp.maximum(s - 1, 0), nloc - 1), s > 0
+                elif j == nloc + 1:
+                    cell, on = cell_of(jnp.minimum(s + 1, ntrack - 1), 0), s < ntrack - 1
+                else:
+                    cell, on = cell_of(s, j - 1), True
+                at = lax.rem(cell, LANES)
+                start = pl.multiple_of((cell // LANES) * LANES, LANES)
+                moved = pltpu.roll(sums[k], lax.rem(at + LANES - j, LANES), 1)
+                hit = lane == jnp.where(on, at, -1)
+                acc[k, :, pl.ds(start, LANES)] += jnp.where(hit, moved, 0.0)
         return carry
 
-    lax.fori_loop(0, ntrack, segment, 0)
-
-
-def whole(shape):
-    return pl.BlockSpec(shape, lambda *_: (0,) * len(shape))
+    lax.fori_loop(0, ntrack // 2, two, 0)
+    writes = []
+    for part in range(parts):
+        rows = pl.ds(part * SUBLANES, SUBLANES)
+        acc[0, rows] += acc[1, rows]
+        writes.append(pltpu.make_async_copy(acc.at[0, rows], out_hbm.at[rows], out_sems.at[part]))
+        writes[-1].start()
+    for write in writes:
+        write.wait()
 
 
 def on_device(slowness_cells, cell_of_group, taper, secant, primary, quadrature, observed):
@@ -284,6 +295,7 @@
     vmem = pl.BlockSpec(memory_space=pltpu.VMEM)
     hbm = pl.BlockSpec(memory_space=pl.ANY)
 
+    cells = pltpu.with_memory_space_constraint(cell_of_group, pltpu.HBM)
     even = lax.ppermute(cell_of_group, "track", pairs(ntrack, 0))
     odd = lax.ppermute(cell_of_group, "track", pairs(ntrack, 1))
     cum, total = pl.pallas_call(
@@ -298,7 +310,7 @@
         compiler_params=pltpu.CompilerParams(vmem_limit_bytes=4 * MIB),
         cost_estimate=pl.CostEstimate(flops=10**11, bytes_accessed=10**7, transcendentals=0),
         name="gather",
-    )(cell_of_group, even, odd, slowness_cells)
+    )(cells, even, odd, pltpu.with_memory_space_constraint(slowness_cells, pltpu.HBM))
     totals = [
         lax.ppermute(total, "depth", [(i, i ^ k) for i in range(ndepth)]) for k in range(1, ndepth)
     ]
@@ -324,18 +336,20 @@
         ],
         compiler_params=pltpu.CompilerParams(vmem_limit_bytes=20 * MIB),
         name="focus",
-    )(*totals, cell_of_group, cum, taper.T, secant.reshape(1, angles), observed, primary, quadrature)
+    )(*totals, cells, cum, taper.T, secant.reshape(1, angles), observed, primary, quadrature)
     all_sums = lax.all_to_all(jnp.broadcast_to(sums[None], (ndev,) + sums.shape), axes, 0, 0)
 
     gradient = pl.pallas_call(
         functools.partial(scatter_kernel, nloc, ndepth, ntrack),
         out_shape=f32((depth, ncells)),
         in_specs=[vmem],
-        out_specs=vmem,
+        out_specs=hbm,
         scratch_shapes=[
+            pltpu.VMEM((2, depth, ncells), jnp.float32),
             pltpu.VMEM((SUBLANES * ntrack, LANES), jnp.int32),
             pltpu.SMEM((SUBLANES * ntrack, LANES), jnp.int32),
             pltpu.SemaphoreType.DMA,
+            pltpu.SemaphoreType.DMA((depth // SUBLANES,)),
         ],
         compiler_params=pltpu.CompilerParams(vmem_limit_bytes=60 * MIB),
         name="scatter",

time: 50.8 us -> 48.7 us (0.959)
  local copies, waits for them, and re-layouts: 2.28 us -> 0.03 us
    unnamed x16 -> x10, local copies, waits for them, and re-layouts: 2.27 us -> 0.02 us
    pallas_call x1, Pallas kernels: 2.4 us -> 3 us  [on_device(): pl.pallas_call(functools.partial(gather_kernel, nloc, ntrack), out_shape=...]
where the time goes in v3:
time: 48.7 us; the launch traced here: 48.4 us
  Pallas kernels  21.2 us (44%)
  blocking collectives  13.4 us (28%)
  starting transfers between devices  9.06 us (19%)
  waiting for transfers between devices  4.02 us (8%)
  between operations  0.73 us (1%)
    all_to_all x1, blocking collectives, on_device(): lax.all_to_all(jnp.broadcast_to(sums[None], (ndev,) + sums.shape), axes,...  13.4 us
    pallas_call x1, Pallas kernels, on_device(): pl.pallas_call(functools.partial(focus_kernel, nloc, group, reach, ndepth...  12.9 us
    pallas_call x1, Pallas kernels, on_device(): pl.pallas_call(functools.partial(scatter_kernel, nloc, ndepth, ntrack), o...  5.26 us
    ppermute x1, starting transfers between devices, on_device(): even = lax.ppermute(cell_of_group, 'track', pairs(ntrack, 0))  4.72 us
    ppermute x3, starting transfers between devices, on_device(): lax.ppermute(total, 'depth', [(i, i ^ k) for i in range(ndepth)])  3.55 us
    ppermute x3, waiting for transfers between devices, on_device(): lax.ppermute(total, 'depth', [(i, i ^ k) for i in range(ndepth)])  3.07 us
    pallas_call x1, Pallas kernels, on_device(): pl.pallas_call(functools.partial(gather_kernel, nloc, ntrack), out_shape=...  3 us
  transfers between devices with their start and end apart: 5, of which 4 were waited for; matrix products, arithmetic and copies ran while one was open for 0% of the time, Pallas kernels for 0%

profile of v3, /device:TPU:0, one launch (start us, length us, event | category | flops | bytes accessed | tf_op | source)
XLA Modules:
  0.0 48.4 jit_solution(9631511241430304565)
XLA Ops:
  0.6 0.0 copy-start.2
  0.6 0.0 copy-start.1
  0.7 0.0 copy-start
  0.7 0.0 copy-start.4
  0.7 0.0 copy-start.3
  0.7 0.8 %collective-permute-start.1 = (s32[16]{0:T(128)}, s32[16]{0:T(128)S(1)}, u32[]{:S(2)}, u32[]{:S(2)}) collective-permute-start(s32[16]{0:T(128)} %refs_3_.1), channel_id=1, source_target_pairs={{1,2},{3,4},{5,6},{2,1},{4,3},{6,5},{9,10},{11,12},{13,14},{10,9},... | collective-permute-start | bytes 200 | tf_op jit(solution)/shard_map/ppermute | solution.py:300
  1.5 4.7 %collective-permute-start = (s32[16]{0:T(128)}, s32[16]{0:T(128)S(1)}, u32[]{:S(2)}, u32[]{:S(2)}) collective-permute-start(s32[16]{0:T(128)} %refs_3_.1), channel_id=1, source_target_pairs={{0,1},{2,3},{4,5},{6,7},{1,0},{3,2},{5,4},{7,6},{8,9},{10,11},{12,... | collective-permute-start | bytes 200 | tf_op jit(solution)/shard_map/ppermute | solution.py:299
  6.2 0.0 collective-permute-done.1.odd_ref
  6.2 0.9 %collective-permute-done.even_ref = s32[16]{0:T(128)S(1)} collective-permute-done((s32[16]{0:T(128)}, s32[16]{0:T(128)S(1)}, u32[]{:S(2)}, u32[]{:S(2)}) %collective-permute-start) | collective-permute-done | bytes 96 | tf_op jit(solution)/shard_map/ppermute | solution.py:299
  7.2 3.0 %gather.1 = (f32[32,128]{1,0:T(8,128)S(1)}, f32[8,128]{1,0:T(8,128)S(1)}) custom-call(s32[16]{0:T(128)} %refs_3_.1, s32[16]{0:T(128)S(1)} %collective-permute-done.even_ref, s32[16]{0:T(128)S(1)} %collective-permute-done.1.odd_ref, f32[32,16384]{1,0:T(8,128)} %slow_ref.1), custom_call_target="tpu_custom_call" | custom-call | flops 99999997952 | bytes 10000000 | tf_op jit(solution)/shard_map/gather/pallas_call | solution.py:301
  10.2 2.5 %collective-permute-start.4 = (f32[8,128]{1,0:T(8,128)S(1)}, f32[8,128]{1,0:T(8,128)S(1)}, u32[]{:S(2)}, u32[]{:S(2)}) collective-permute-start(f32[8,128]{1,0:T(8,128)S(1)} %get-tuple-element.6), channel_id=1, source_target_pairs={{0,24},{8,16},{16,8},{24,0},{1,25},{9,17},{17,9},{25,1},{2,26},{10... | collective-permute-start | bytes 12296 | tf_op jit(solution)/shard_map/ppermute | solution.py:315
  12.7 0.5 %collective-permute-start.3 = (f32[8,128]{1,0:T(8,128)S(1)}, f32[8,128]{1,0:T(8,128)S(1)}, u32[]{:S(2)}, u32[]{:S(2)}) collective-permute-start(f32[8,128]{1,0:T(8,128)S(1)} %get-tuple-element.6), channel_id=1, source_target_pairs={{0,16},{8,24},{16,0},{24,8},{1,17},{9,25},{17,1},{25,9},{2,18},{10... | collective-permute-start | bytes 12296 | tf_op jit(solution)/shard_map/ppermute | solution.py:315
  13.2 0.5 %collective-permute-start.2 = (f32[8,128]{1,0:T(8,128)S(1)}, f32[8,128]{1,0:T(8,128)S(1)}, u32[]{:S(2)}, u32[]{:S(2)}) collective-permute-start(f32[8,128]{1,0:T(8,128)S(1)} %get-tuple-element.6), channel_id=1, source_target_pairs={{0,8},{8,0},{16,24},{24,16},{1,9},{9,1},{17,25},{25,17},{2,10},{10... | collective-permute-start | bytes 12296 | tf_op jit(solution)/shard_map/ppermute | solution.py:315
  13.7 1.0 %collective-permute-done.4.refs_2_ = f32[8,128]{1,0:T(8,128)S(1)} collective-permute-done((f32[8,128]{1,0:T(8,128)S(1)}, f32[8,128]{1,0:T(8,128)S(1)}, u32[]{:S(2)}, u32[]{:S(2)}) %collective-permute-start.4) | collective-permute-done | bytes 4128 | tf_op jit(solution)/shard_map/ppermute | solution.py:315
  14.7 1.5 %collective-permute-done.3.refs_1_ = f32[8,128]{1,0:T(8,128)S(1)} collective-permute-done((f32[8,128]{1,0:T(8,128)S(1)}, f32[8,128]{1,0:T(8,128)S(1)}, u32[]{:S(2)}, u32[]{:S(2)}) %collective-permute-start.3) | collective-permute-done | bytes 4128 | tf_op jit(solution)/shard_map/ppermute | solution.py:315
  16.3 0.5 %collective-permute-done.2.refs_0_ = f32[8,128]{1,0:T(8,128)S(1)} collective-permute-done((f32[8,128]{1,0:T(8,128)S(1)}, f32[8,128]{1,0:T(8,128)S(1)}, u32[]{:S(2)}, u32[]{:S(2)}) %collective-permute-start.2) | collective-permute-done | bytes 4128 | tf_op jit(solution)/shard_map/ppermute | solution.py:315
  16.8 0.0 copy-done.2
  16.8 0.0 copy-done.1
  16.8 0.0 copy-done
  16.8 0.0 copy-done.4
  16.8 0.0 copy-done.3
  16.8 12.9 %focus.1 = (f32[32,512]{1,0:T(8,128)}, f32[8,128]{1,0:T(8,128)S(1)}) custom-call(f32[8,128]{1,0:T(8,128)S(1)} %collective-permute-done.2.refs_0_, f32[8,128]{1,0:T(8,128)S(1)} %collective-permute-done.3.refs_1_, f32[8,128]{1,0:T(8,128)S(1)} %collective-permute-done.4.refs_2_, s32[16]{0:T(128)} %refs_3_.1, f32[32,128]{1,0:T(8,128)S(1)} %get-tuple-element.7.refs_4_, ...), custom_call_target="tpu_custom_call" | custom-call | tf_op jit(solution)/shard_map/focus/pallas_call | solution.py:317
  29.8 13.4 %all_to_all.5.m_ref = f32[32,8,128]{2,1,0:T(8,128)} all-to-all(f32[32,8,128]{2,1,0:T(8,128)S(1)} %broadcast_in_dim.2), channel_id=1, replica_groups=mesh['depth'=4,'track'=8] {'depth','track'}, dimensions={0} | all-to-all | bytes 262144 | tf_op jit(solution)/shard_map/all_to_all | solution.py:340
  43.2 5.3 %scatter.1 = f32[32,16384]{1,0:T(8,128)} custom-call(f32[32,8,128]{2,1,0:T(8,128)} %all_to_all.5.m_ref), custom_call_target="tpu_custom_call" | custom-call | tf_op jit(solution)/shard_map/scatter/pallas_call | solution.py:342
  (1 shorter events, 0.0 us)
Async XLA Ops:
  0.6 16.2 %copy-start.2 = (f32[32,512]{1,0:T(8,128)S(1)}, f32[32,512]{1,0:T(8,128)}, u32[]{:S(2)}) copy-start(f32[32,512]{1,0:T(8,128)} %refs_7_.1) | copy-start | bytes 196612
  0.6 16.2 %copy-start.1 = (bf16[32,512,256]{2,1,0:T(8,128)(2,1)S(1)}, bf16[32,512,256]{2,1,0:T(8,128)(2,1)}, u32[]{:S(2)}) copy-start(bf16[32,512,256]{2,1,0:T(8,128)(2,1)} %refs_9_.1) | copy-start | bytes 25165828
  0.7 16.1 %copy-start = (bf16[32,512,256]{2,1,0:T(8,128)(2,1)S(1)}, bf16[32,512,256]{2,1,0:T(8,128)(2,1)}, u32[]{:S(2)}) copy-start(bf16[32,512,256]{2,1,0:T(8,128)(2,1)} %refs_8_.1) | copy-start | bytes 25165828
  0.7 16.1 %copy-start.4 = (f32[256]{0:T(256)S(1)}, f32[256]{0:T(256)}, u32[]{:S(2)}) copy-start(f32[256]{0:T(256)} %param.10) | copy-start | bytes 3076
  0.7 16.1 %copy-start.3 = (f32[256,9]{0,1:T(8,128)S(1)}, f32[256,9]{0,1:T(8,128)}, u32[]{:S(2)}) copy-start(f32[256,9]{0,1:T(8,128)} %param.9) | copy-start | bytes 27652
  0.7 5.5 %collective-permute-start.1 = (s32[16]{0:T(128)}, s32[16]{0:T(128)S(1)}, u32[]{:S(2)}, u32[]{:S(2)}) collective-permute-start(s32[16]{0:T(128)} %refs_3_.1), channel_id=1, source_target_pairs={{1,2},{3,4},{5,6},{2,1},{4,3},{6,5},{9,10},{11,12},{13,14},{10,9},... | collective-permute-start | bytes 200 | tf_op jit(solution)/shard_map/ppermute | solution.py:300
  1.5 5.7 %collective-permute-start = (s32[16]{0:T(128)}, s32[16]{0:T(128)S(1)}, u32[]{:S(2)}, u32[]{:S(2)}) collective-permute-start(s32[16]{0:T(128)} %refs_3_.1), channel_id=1, source_target_pairs={{0,1},{2,3},{4,5},{6,7},{1,0},{3,2},{5,4},{7,6},{8,9},{10,11},{12,... | collective-permute-start | bytes 200 | tf_op jit(solution)/shard_map/ppermute | solution.py:299
  10.2 4.6 %collective-permute-start.4 = (f32[8,128]{1,0:T(8,128)S(1)}, f32[8,128]{1,0:T(8,128)S(1)}, u32[]{:S(2)}, u32[]{:S(2)}) collective-permute-start(f32[8,128]{1,0:T(8,128)S(1)} %get-tuple-element.6), channel_id=1, source_target_pairs={{0,24},{8,16},{16,8},{24,0},{1,25},{9,17},{17,9},{25,1},{2,26},{10... | collective-permute-start | bytes 12296 | tf_op jit(solution)/shard_map/ppermute | solution.py:315
  12.7 3.6 %collective-permute-start.3 = (f32[8,128]{1,0:T(8,128)S(1)}, f32[8,128]{1,0:T(8,128)S(1)}, u32[]{:S(2)}, u32[]{:S(2)}) collective-permute-start(f32[8,128]{1,0:T(8,128)S(1)} %get-tuple-element.6), channel_id=1, source_target_pairs={{0,16},{8,24},{16,0},{24,8},{1,17},{9,25},{17,1},{25,9},{2,18},{10... | collective-permute-start | bytes 12296 | tf_op jit(solution)/shard_map/ppermute | solution.py:315
  13.2 3.6 %collective-permute-start.2 = (f32[8,128]{1,0:T(8,128)S(1)}, f32[8,128]{1,0:T(8,128)S(1)}, u32[]{:S(2)}, u32[]{:S(2)}) collective-permute-start(f32[8,128]{1,0:T(8,128)S(1)} %get-tuple-element.6), channel_id=1, source_target_pairs={{0,8},{8,0},{16,24},{24,16},{1,9},{9,1},{17,25},{25,17},{2,10},{10... | collective-permute-start | bytes 12296 | tf_op jit(solution)/shard_map/ppermute | solution.py:315
